TPU v7x, 32 devices: a whole 2x2x4 slice. The times are simulated.
32 devices in a mesh: seq: 16 (over z, y, x), head: 2 (over core).
Axes of the slice: x: 2, y: 2, z: 4, core: 2. Of those that a mesh axis runs over, the one named last changes fastest.
Arguments:
- block_input: bfloat16 [4096, 1024], P('seq'), may hold values from -6 to 6
- value_first: bfloat16 [4096, 1024], P('seq', 'head'), may hold values from -6 to 6
- out_cotangent: bfloat16 [4096, 1024], P('seq'), may hold values from -6 to 6
- seq_lengths: int32 [2], replicated, may hold values from 1 to 40, 64 in all
- w_rkv: bfloat16 [3, 1024, 1024], P(None, 'seq', 'head'), may hold values from -0.1875 to 0.1875
- w_out: bfloat16 [1024, 1024], P('head', 'seq'), may hold values from -0.375 to 0.375
- ffn_key: bfloat16 [4096, 1024], P('head', 'seq'), may hold values from -0.1875 to 0.1875
- ffn_value: bfloat16 [4096, 1024], P('head', 'seq'), may hold values from -0.09375 to 0.09375
- channel_params: bfloat16 [19, 1024], P(None, 'seq'), may hold values from -7 to 2, as said below
- low_rank: bfloat16 [576, 1024], P(None, 'seq'), may hold values from -1.1 to 1.1, as said below
Outputs:
- block_output: bfloat16 [4096, 1024], P('seq')
- input_grad: float32 [4096, 1024], P('seq')
- value_first_grad: float32 [4096, 1024], P('seq', 'head')
- w_rkv_grad: float32 [3, 1024, 1024], P(None, 'seq', 'head')
- w_out_grad: float32 [1024, 1024], P('head', 'seq')
- ffn_key_grad: float32 [4096, 1024], P('head', 'seq')
- ffn_value_grad: float32 [4096, 1024], P('head', 'seq')
- channel_params_grad: float32 [19, 1024], P(None, ('seq', 'head'))
- low_rank_grad: float32 [576, 1024], P(None, ('seq', 'head'))
Inputs may be any that keep to these rules, and one draw needn't show every extreme that they name: `seq_lengths`: 2 sequence lengths counted in blocks of 64 tokens, summing to 64; the longest has 40 blocks. `channel_params`: rows 0 to 3: layer norms' gains and biases; 4 to 10: token-shift coefficients; 11: decay bias; 12: rate bias; 13: value-first bias; 14: key normalization scale; 15: key rate scale; 16: bonus scale; 17, 18: group norm gain and bias. `low_rank`: rows 0 to 287 map features to the decay, rate, value-first and gate ranks in that order; the next 288 rows map those ranks back to features.
All inputs are finite; a program needn't handle non-finite values.
Results may differ from a plain program's by a relative error of at most 0.017.
Values may be sent and summed in bfloat16 or wider, within the bound.
A program may use at most 320 MiB of HBM per device.

v0:
```python
from functools import partial

import jax
import jax.numpy as jnp
from jax import lax
from jax.sharding import PartitionSpec as P

HEAD_SIZE = 64
DECAY_RANK = 64
RATE_RANK = 64
VALUE_RANK = 32
RANKS = 288
SPAN = 64


norm_eps = 1e-05
group_eps = 0.00064
key_eps = 1e-06
highest = lax.Precision.HIGHEST


def shifted(array, axis, by):
    size = lax.axis_size(axis)
    pairs = [(i, i + by) for i in range(size) if 0 <= i + by < size]
    return lax.ppermute(array, axis, pairs)


def prefix(array, axis, join, neutral):
    place = lax.axis_index(axis)
    gathered = jax.tree.map(
        lambda a, kind: lax.all_gather(a.astype(kind), axis), array, (jnp.bfloat16, jnp.bfloat16)
    )
    state = jax.tree.map(lambda a, e: jnp.zeros_like(a) + jnp.asarray(e, a.dtype), array, neutral)

    def one(turn, state):
        return join(
            state,
            jax.tree.map(
                lambda a, own: lax.dynamic_index_in_dim(a, turn, 0, False).astype(own.dtype),
                gathered,
                array,
            ),
        )

    return lax.fori_loop(0, place, one, state)


def prefix_2(array, axis, join, neutral):
    count = lax.axis_size(axis)
    place = lax.axis_index(axis)
    ahead = count - 1 - place
    gathered = jax.tree.map(
        lambda a, kind: lax.all_gather(a.astype(kind), axis),
        array,
        jax.tree.map(lambda a: jnp.bfloat16 if a.dtype == jnp.float32 else a.dtype, array),
    )
    state = jax.tree.map(lambda a, e: jnp.zeros_like(a) + jnp.asarray(e, a.dtype), array, neutral)

    def one(turn, state):
        source = count - 1 - turn
        return join(
            state,
            jax.tree.map(
                lambda a, own: lax.dynamic_index_in_dim(a, source, 0, False).astype(own.dtype),
                gathered,
                array,
            ),
        )

    return lax.fori_loop(0, ahead, one, state)


def dot_plain(left, right):
    return jnp.dot(left, right, preferred_element_type=jnp.float32)


def dot_rows(left, right):
    return lax.dot_general(
        left, right, (((1,), (1,)), ((), ())), preferred_element_type=jnp.float32
    )


def dot_tokens(left, right):
    return lax.dot_general(
        left, right, (((0,), (0,)), ((), ())), preferred_element_type=jnp.float32
    )


def dot_high(left, right):
    return jnp.dot(left, right, precision=highest, preferred_element_type=jnp.float32)


def tokens_high(left, right):
    return lax.dot_general(
        left, right, (((0,), (0,)), ((), ())), precision=highest, preferred_element_type=jnp.float32
    )


def layer_norm(inputs, gain, bias):
    centre = inputs - jnp.mean(inputs, axis=-1, keepdims=True)
    spread = jnp.mean(centre * centre, axis=-1, keepdims=True)
    return centre * lax.rsqrt(spread + norm_eps) * gain + bias


def divide_into_attention_parts(member, channels_per_attention_part):
    return member.reshape(
        member.shape[0], member.shape[1] // channels_per_attention_part, channels_per_attention_part
    )


def prepare(
    lookup_vector_mapped,
    payload_vector_mapped,
    first_layer_values_vector,
    forgetting_preactivation,
    learning_speed_preactivation,
    interpolation_preactivation,
    lookup_multiplier_vector,
    lookup_learning_coefficient,
    channels_per_attention_part,
):
    decay_rate = jnp.exp(-jnp.exp(-jax.nn.softplus(-forgetting_preactivation) - 0.5))
    in_rate = jax.nn.sigmoid(learning_speed_preactivation)
    payload_vector_combined = payload_vector_mapped + (
        first_layer_values_vector - payload_vector_mapped
    ) * jax.nn.sigmoid(interpolation_preactivation)
    key_unit = divide_into_attention_parts(
        lookup_vector_mapped * lookup_multiplier_vector, channels_per_attention_part
    )
    key_unit = key_unit * lax.rsqrt(jnp.sum(key_unit * key_unit, axis=-1, keepdims=True) + key_eps)
    key_unit = key_unit.reshape(lookup_vector_mapped.shape)
    key_taken = key_unit * in_rate
    lookup_vector_modified = lookup_vector_mapped * (
        1.0 + (in_rate - 1.0) * lookup_learning_coefficient
    )
    return (decay_rate, key_unit, key_taken, payload_vector_combined, lookup_vector_modified)


def to_spans(member, channels_per_attention_part):
    spans = member.shape[0] // SPAN
    return jnp.transpose(
        member.reshape(
            spans, SPAN, member.shape[1] // channels_per_attention_part, channels_per_attention_part
        ),
        (0, 2, 1, 3),
    )


def span_parts(decay_rate, key_unit, key_taken, payload_vector_combined, lookup_vector_modified):
    length = decay_rate.shape[2]
    log_decay = jnp.log(decay_rate)
    log_total = jnp.cumsum(log_decay, axis=2)
    gamma = jnp.exp(log_total)
    before = jnp.exp(log_total - log_decay)
    inverse = jnp.exp(-log_total)
    unit_back = key_unit * before
    key_hat = lookup_vector_modified * inverse
    taken_hat = key_taken * inverse
    strict = jnp.tril(jnp.ones((length, length), jnp.float32), -1)
    cross_taken = jnp.einsum("zhtn,zhsn->zhts", unit_back, taken_hat, precision=highest) * strict
    cross_key = jnp.einsum("zhtn,zhsn->zhts", unit_back, key_hat, precision=highest) * strict
    system = cross_taken + jnp.eye(length, dtype=jnp.float32)
    carried = jax.scipy.linalg.solve_triangular(system, unit_back, lower=True, unit_diagonal=True)
    source = jnp.einsum("zhts,zhsv->zhtv", cross_key, payload_vector_combined, precision=highest)
    base = jax.scipy.linalg.solve_triangular(system, source, lower=True, unit_diagonal=True)
    return (gamma, key_hat, taken_hat, carried, base)


def previous_position_interpolation(
    sequence_restart_markers,
    memory_matrix_before,
    query_vector_lines,
    lookup_vector_mapped,
    payload_vector_mapped,
    first_layer_values_vector,
    forgetting_preactivation,
    learning_speed_preactivation,
    interpolation_preactivation,
    emission_sigmoid_multiplier,
    lookup_multiplier_vector,
    lookup_learning_coefficient,
    extra_diagonal_coefficient,
    channel_gain_after_standardize,
    channel_offset_after_standardize,
):
    channels_per_attention_part = memory_matrix_before.shape[-1]
    tokens_dev = query_vector_lines.shape[0]
    spans = tokens_dev // SPAN
    decay_rate, key_unit, key_taken, payload_vector_combined, lookup_vector_modified = prepare(
        lookup_vector_mapped,
        payload_vector_mapped,
        first_layer_values_vector,
        forgetting_preactivation,
        learning_speed_preactivation,
        interpolation_preactivation,
        lookup_multiplier_vector,
        lookup_learning_coefficient,
        channels_per_attention_part,
    )
    value_spans = to_spans(payload_vector_combined, channels_per_attention_part)
    gamma, key_hat, taken_hat, carried, base = span_parts(
        to_spans(decay_rate, channels_per_attention_part),
        to_spans(key_unit, channels_per_attention_part),
        to_spans(key_taken, channels_per_attention_part),
        value_spans,
        to_spans(lookup_vector_modified, channels_per_attention_part),
    )
    recept_tilde = to_spans(query_vector_lines, channels_per_attention_part) * gamma
    inclusive = jnp.tril(jnp.ones((SPAN, SPAN), jnp.float32))
    read_key = jnp.einsum("zhtn,zhsn->zhts", recept_tilde, key_hat, precision=highest) * inclusive
    read_taken = (
        jnp.einsum("zhtn,zhsn->zhts", recept_tilde, taken_hat, precision=highest) * inclusive
    )
    keep_first = 1.0 - sequence_restart_markers.reshape(spans, SPAN)[:, 0]
    span_end = gamma[:, :, -1, :]

    def advance(state_now, items):
        (
            keep_now,
            carried_now,
            base_now,
            tilde_now,
            rk_now,
            rt_now,
            value_now,
            key_now,
            taken_now,
            end_now,
        ) = items
        state_now = state_now * keep_now
        along = base_now + jnp.einsum("htk,hvk->htv", carried_now, state_now, precision=highest)
        read_now = (
            jnp.einsum("hvk,htk->htv", state_now, tilde_now, precision=highest)
            + jnp.einsum("hts,hsv->htv", rk_now, value_now, precision=highest)
            - jnp.einsum("hts,hsv->htv", rt_now, along, precision=highest)
        )
        fresh = jnp.einsum("hsv,hsk->hvk", value_now, key_now, precision=highest) - jnp.einsum(
            "hsv,hsk->hvk", along, taken_now, precision=highest
        )
        state_now = (state_now + fresh) * end_now[:, None, :]
        return (state_now, read_now)

    state_out, reads = lax.scan(
        advance,
        memory_matrix_before,
        (
            keep_first,
            carried,
            base,
            recept_tilde,
            read_key,
            read_taken,
            value_spans,
            key_hat,
            taken_hat,
            span_end,
        ),
    )
    read_out = jnp.transpose(reads, (0, 2, 1, 3)).reshape(
        tokens_dev, -1, channels_per_attention_part
    )
    centre = read_out - jnp.mean(read_out, axis=-1, keepdims=True)
    spread = jnp.mean(centre * centre, axis=-1, keepdims=True)
    standardized_layer_entry = centre * lax.rsqrt(spread + group_eps) * divide_into_attention_parts(
        channel_gain_after_standardize[None, :], channels_per_attention_part
    ) + divide_into_attention_parts(
        channel_offset_after_standardize[None, :], channels_per_attention_part
    )
    extra_diagonal_contribution = jnp.sum(
        divide_into_attention_parts(
            query_vector_lines * lookup_vector_modified * extra_diagonal_coefficient,
            channels_per_attention_part,
        ),
        axis=-1,
        keepdims=True,
    ) * divide_into_attention_parts(payload_vector_combined, channels_per_attention_part)
    attention_branch_outcome = (standardized_layer_entry + extra_diagonal_contribution).reshape(
        query_vector_lines.shape
    ) * emission_sigmoid_multiplier
    return (attention_branch_outcome, state_out)


def compose(earlier, later):
    matrix = jnp.einsum("hij,hjk->hik", earlier[0], later[0], precision=highest)
    offset_state = jnp.einsum("hij,hjk->hik", earlier[1], later[0], precision=highest) + later[1]
    return (matrix, offset_state)


def transition(
    sequence_restart_markers,
    decay_rate,
    key_unit,
    key_taken,
    payload_vector_combined,
    lookup_vector_modified,
    channels_per_attention_part,
):
    spans = decay_rate.shape[0] // SPAN
    heads_dev = decay_rate.shape[1] // channels_per_attention_part
    value_spans = to_spans(payload_vector_combined, channels_per_attention_part)
    gamma, key_hat, taken_hat, carried, base = span_parts(
        to_spans(decay_rate, channels_per_attention_part),
        to_spans(key_unit, channels_per_attention_part),
        to_spans(key_taken, channels_per_attention_part),
        value_spans,
        to_spans(lookup_vector_modified, channels_per_attention_part),
    )
    span_end = gamma[:, :, -1, :]
    keep_first = 1.0 - sequence_restart_markers.reshape(spans, SPAN)[:, 0]
    unit_mat = jnp.broadcast_to(
        jnp.eye(channels_per_attention_part, dtype=jnp.float32),
        (heads_dev, channels_per_attention_part, channels_per_attention_part),
    )
    span_mats = (
        (unit_mat[None] - jnp.einsum("zhsk,zhsj->zhkj", carried, taken_hat, precision=highest))
        * span_end[:, :, None, :]
        * keep_first[:, None, None, None]
    )
    span_offsets = (
        jnp.einsum("zhsv,zhsk->zhvk", value_spans, key_hat, precision=highest)
        - jnp.einsum("zhsv,zhsk->zhvk", base, taken_hat, precision=highest)
    ) * span_end[:, :, None, :]

    def fold(carry, items):
        return (compose(carry, items), None)

    (matrix, offset_state), _ = lax.scan(
        fold, (unit_mat, jnp.zeros_like(unit_mat)), (span_mats, span_offsets)
    )
    return (matrix, offset_state)


def project(mixed_rows, rkv_cols, maps_in, maps_out, chan_params):
    first_end = DECAY_RANK
    second_end = first_end + RATE_RANK
    third_end = second_end + VALUE_RANK
    query_vector_lines = dot_plain(mixed_rows[0], rkv_cols[0])
    lookup_vector_mapped = dot_plain(mixed_rows[2], rkv_cols[1])
    payload_vector_mapped = dot_plain(mixed_rows[3], rkv_cols[2])
    decay_hidden = jnp.tanh(dot_rows(mixed_rows[1], maps_in[:first_end]))
    decay_low = decay_hidden.astype(jnp.bfloat16)
    forgetting_preactivation = chan_params[11] + dot_plain(decay_low, maps_out[:first_end])
    rate_low = dot_rows(mixed_rows[4], maps_in[first_end:second_end]).astype(jnp.bfloat16)
    learning_speed_preactivation = chan_params[12] + dot_plain(
        rate_low, maps_out[first_end:second_end]
    )
    mix_low = dot_rows(mixed_rows[3], maps_in[second_end:third_end]).astype(jnp.bfloat16)
    interpolation_preactivation = chan_params[13] + dot_plain(
        mix_low, maps_out[second_end:third_end]
    )
    gate_hidden = jax.nn.sigmoid(dot_rows(mixed_rows[5], maps_in[third_end:]))
    gate_low = gate_hidden.astype(jnp.bfloat16)
    emission_sigmoid_multiplier = dot_plain(gate_low, maps_out[third_end:])
    saved = (decay_hidden, decay_low, rate_low, mix_low, gate_hidden, gate_low)
    return (
        saved,
        (
            query_vector_lines,
            lookup_vector_mapped,
            payload_vector_mapped,
            forgetting_preactivation,
            learning_speed_preactivation,
            interpolation_preactivation,
            emission_sigmoid_multiplier,
        ),
    )


def project_back(mixed_rows, rkv_cols, maps_in, maps_out, saved, grads_in):
    first_end = DECAY_RANK
    second_end = first_end + RATE_RANK
    third_end = second_end + VALUE_RANK
    decay_hidden, decay_low, rate_low, mix_low, gate_hidden, gate_low = saved
    d_recept, d_key, d_value, d_decay, d_rate, d_mix, d_gate = grads_in
    recept_low = d_recept.astype(jnp.bfloat16)
    key_low = d_key.astype(jnp.bfloat16)
    value_low = d_value.astype(jnp.bfloat16)
    rkv_grad = jnp.stack(
        [
            dot_tokens(mixed_rows[0], recept_low),
            dot_tokens(mixed_rows[2], key_low),
            dot_tokens(mixed_rows[3], value_low),
        ]
    )
    maps_float = maps_in.astype(jnp.float32)
    decay_back = d_decay.astype(jnp.bfloat16)
    decay_rank = dot_rows(decay_back, maps_out[:first_end]) * (1.0 - decay_hidden * decay_hidden)
    rate_back = d_rate.astype(jnp.bfloat16)
    rate_rank = dot_rows(rate_back, maps_out[first_end:second_end])
    mix_back_low = d_mix.astype(jnp.bfloat16)
    mix_rank = dot_rows(mix_back_low, maps_out[second_end:third_end])
    gate_back = d_gate.astype(jnp.bfloat16)
    gate_rank = dot_rows(gate_back, maps_out[third_end:]) * gate_hidden * (1.0 - gate_hidden)
    out_grads = jnp.concatenate(
        [
            dot_tokens(decay_low, decay_back),
            dot_tokens(rate_low, rate_back),
            dot_tokens(mix_low, mix_back_low),
            dot_tokens(gate_low, gate_back),
        ],
        axis=0,
    )
    in_grads = jnp.concatenate(
        [
            tokens_high(decay_rank, mixed_rows[1].astype(jnp.float32)),
            tokens_high(rate_rank, mixed_rows[4].astype(jnp.float32)),
            tokens_high(mix_rank, mixed_rows[3].astype(jnp.float32)),
            tokens_high(gate_rank, mixed_rows[5].astype(jnp.float32)),
        ],
        axis=0,
    )
    grad_recept = dot_rows(recept_low, rkv_cols[0])
    grad_decay = dot_high(decay_rank, maps_float[:first_end])
    grad_key = dot_rows(key_low, rkv_cols[1])
    grad_value = dot_rows(value_low, rkv_cols[2]) + dot_high(
        mix_rank, maps_float[second_end:third_end]
    )
    grad_rate = dot_high(rate_rank, maps_float[first_end:second_end])
    grad_gate = dot_high(gate_rank, maps_float[third_end:])
    bias_grads = jnp.stack(
        [jnp.sum(d_decay, axis=0), jnp.sum(d_rate, axis=0), jnp.sum(d_mix, axis=0)]
    )
    return (
        [grad_recept, grad_decay, grad_key, grad_value, grad_rate, grad_gate],
        rkv_grad,
        in_grads,
        out_grads,
        bias_grads,
    )


def shift_diff(standardized_layer_entry, edge_row, keep_mask):
    previous = jnp.concatenate([edge_row, standardized_layer_entry[:-1]], axis=0) * keep_mask
    return previous - standardized_layer_entry


def mix_back(grads_list, coeffs, shifted_diff, keep_mask):
    direct = jnp.zeros_like(shifted_diff)
    carried = jnp.zeros_like(shifted_diff)
    for column, grad_rows in enumerate(grads_list):
        direct = direct + grad_rows * (1.0 - coeffs[column])
        carried = carried + grad_rows * coeffs[column]
    coeff_grads = jnp.stack([jnp.sum(grad_rows * shifted_diff, axis=0) for grad_rows in grads_list])
    return (direct, carried * keep_mask, coeff_grads)


def reduce_pair(first_grad, second_grad):
    return (
        lax.psum_scatter(first_grad, "seq", scatter_dimension=1, tiled=True),
        lax.psum_scatter(second_grad, "seq", scatter_dimension=1, tiled=True),
    )


def on_device(
    block_input,
    value_first,
    out_cotangent,
    seq_lengths,
    w_rkv,
    w_out,
    ffn_key,
    ffn_value,
    channel_params,
    low_rank,
):
    tokens_dev = block_input.shape[0]
    rkv_all, out_all, key_all, value_all, params_low, ranks_all = (
        lax.all_gather(w_rkv, "seq", axis=1, tiled=True),
        lax.all_gather(w_out, "seq", axis=1, tiled=True),
        lax.all_gather(ffn_key, "seq", axis=1, tiled=True),
        lax.all_gather(ffn_value, "seq", axis=1, tiled=True),
        lax.all_gather(channel_params, "seq", axis=1, tiled=True),
        lax.all_gather(low_rank, "seq", axis=1, tiled=True),
    )
    local_width = rkv_all.shape[2]
    offset = lax.axis_index("head") * local_width
    params = params_low.astype(jnp.float32)
    local_params = lax.dynamic_slice_in_dim(params, offset, local_width, 1)
    maps_in = ranks_all[:RANKS]
    maps_out = lax.dynamic_slice_in_dim(ranks_all[RANKS:], offset, local_width, 1)
    position = lax.axis_index("seq") * tokens_dev + jnp.arange(tokens_dev, dtype=jnp.int32)
    starts = (jnp.cumsum(seq_lengths) - seq_lengths) * SPAN
    sequence_restart_markers = jnp.any(position[:, None] == starts[None, :], axis=1).astype(
        jnp.float32
    )
    keep_mask = (1.0 - sequence_restart_markers)[:, None]
    inputs_float = block_input.astype(jnp.float32)
    normed_one = layer_norm(inputs_float, params[0], params[1])
    edge_one = shifted(normed_one[-1:], "seq", 1)
    diff_one = shift_diff(normed_one, edge_one, keep_mask)
    mixed_rows = [
        (normed_one + diff_one * params[4 + column]).astype(jnp.bfloat16) for column in range(6)
    ]
    saved, mixer_args = project(mixed_rows, rkv_all, maps_in, maps_out, local_params)
    (
        query_vector_lines,
        lookup_vector_mapped,
        payload_vector_mapped,
        forgetting_preactivation,
        learning_speed_preactivation,
        interpolation_preactivation,
        emission_sigmoid_multiplier,
    ) = mixer_args
    first_layer_values_vector = value_first.astype(jnp.float32)
    fixed_params = tuple((local_params[row_index] for row_index in range(14, 19)))
    decay_rate, key_unit, key_taken, payload_vector_combined, lookup_vector_modified = prepare(
        lookup_vector_mapped,
        payload_vector_mapped,
        first_layer_values_vector,
        forgetting_preactivation,
        learning_speed_preactivation,
        interpolation_preactivation,
        fixed_params[0],
        fixed_params[1],
        HEAD_SIZE,
    )
    matrix, offset_state = transition(
        sequence_restart_markers,
        decay_rate,
        key_unit,
        key_taken,
        payload_vector_combined,
        lookup_vector_modified,
        HEAD_SIZE,
    )
    unit_mat = jnp.broadcast_to(jnp.eye(HEAD_SIZE, dtype=jnp.float32), matrix.shape)
    zero_state = jnp.zeros_like(matrix)
    _, memory_matrix_before = prefix((matrix, offset_state), "seq", compose, (unit_mat, zero_state))
    primal_args = (
        memory_matrix_before,
        query_vector_lines,
        lookup_vector_mapped,
        payload_vector_mapped,
        first_layer_values_vector,
        forgetting_preactivation,
        learning_speed_preactivation,
        interpolation_preactivation,
        emission_sigmoid_multiplier,
    ) + fixed_params
    mixer_fn = partial(previous_position_interpolation, sequence_restart_markers)
    (mixer_out, _), mixer_back = jax.vjp(mixer_fn, *primal_args)
    mixer_low = mixer_out.astype(jnp.bfloat16)
    attended = lax.psum(dot_plain(mixer_low, out_all).astype(jnp.bfloat16), "head").astype(
        jnp.float32
    )
    residual_one = inputs_float + attended
    normed_two = layer_norm(residual_one, params[2], params[3])
    edge_two = shifted(normed_two[-1:], "seq", 1)
    diff_two = shift_diff(normed_two, edge_two, keep_mask)
    mixed_ffn = (normed_two + diff_two * params[10]).astype(jnp.bfloat16)
    hidden_pre = dot_rows(mixed_ffn, key_all)
    hidden_low = jnp.square(jax.nn.relu(hidden_pre)).astype(jnp.bfloat16)
    ffn_out = lax.psum(dot_plain(hidden_low, value_all).astype(jnp.bfloat16), "head").astype(
        jnp.float32
    )
    block_output = (residual_one + ffn_out).astype(jnp.bfloat16)
    cot_float = out_cotangent.astype(jnp.float32)
    value_grad = dot_tokens(hidden_low, out_cotangent)
    hidden_grad = dot_rows(out_cotangent, value_all)
    pre_low = (hidden_grad * 2.0 * jax.nn.relu(hidden_pre)).astype(jnp.bfloat16)
    key_grad = dot_tokens(pre_low, mixed_ffn)
    ffn_in_grad = dot_plain(pre_low, key_all)
    direct_two, carried_two, coeff_two = mix_back([ffn_in_grad], params[10:11], diff_two, keep_mask)
    from_next_two = shifted(carried_two[:1], "seq", -1)
    normed_two_grad = direct_two + jnp.concatenate([carried_two[1:], from_next_two], axis=0)
    _, norm_two_back = jax.vjp(layer_norm, residual_one, params[2], params[3])
    resid_part, gain_two, bias_two = norm_two_back(normed_two_grad)
    residual_grad = cot_float + lax.psum(resid_part.astype(jnp.bfloat16), "head").astype(
        jnp.float32
    )
    attend_low = residual_grad.astype(jnp.bfloat16)
    out_grad = dot_tokens(mixer_low, attend_low)
    mixer_grad = dot_rows(attend_low, out_all)
    local_grads = mixer_back((mixer_grad, zero_state))
    _, state_grad = prefix_2(
        (jnp.swapaxes(matrix, 1, 2), local_grads[0]), "seq", compose, (unit_mat, zero_state)
    )
    grads_all = mixer_back((mixer_grad, state_grad))
    d_recept, d_key, d_value, d_first, d_decay, d_rate, d_mix, d_gate = grads_all[1:9]
    param_grads = grads_all[9:]
    mixed_grads, rkv_grad, in_grads, out_grads, bias_grads = project_back(
        mixed_rows,
        rkv_all,
        maps_in,
        maps_out,
        saved,
        (d_recept, d_key, d_value, d_decay, d_rate, d_mix, d_gate),
    )
    direct_one, carried_one, coeff_one = mix_back(mixed_grads, params[4:10], diff_one, keep_mask)
    from_next_one = shifted(carried_one[:1], "seq", -1)
    normed_one_grad = direct_one + jnp.concatenate([carried_one[1:], from_next_one], axis=0)
    _, norm_one_back = jax.vjp(layer_norm, inputs_float, params[0], params[1])
    input_part, gain_one, bias_one = norm_one_back(normed_one_grad)
    input_grad = residual_grad + lax.psum(input_part.astype(jnp.bfloat16), "head").astype(
        jnp.float32
    )
    full_rows = jnp.concatenate(
        [jnp.stack([gain_one, bias_one, gain_two, bias_two]), coeff_one, coeff_two], axis=0
    )
    head_rows = jnp.concatenate([bias_grads, jnp.stack(param_grads)], axis=0)
    placed_rows = lax.dynamic_update_slice_in_dim(
        jnp.zeros((head_rows.shape[0], params.shape[1]), jnp.float32), head_rows, offset, 1
    )
    channel_grad = jnp.concatenate([full_rows, placed_rows], axis=0)
    placed_maps = lax.dynamic_update_slice_in_dim(
        jnp.zeros((out_grads.shape[0], params.shape[1]), jnp.float32), out_grads, offset, 1
    )
    low_rank_grad = jnp.concatenate([in_grads, placed_maps], axis=0)
    channel_shard, low_shard = (
        lax.psum_scatter(channel_grad, ("seq", "head"), scatter_dimension=1, tiled=True),
        lax.psum_scatter(low_rank_grad, ("seq", "head"), scatter_dimension=1, tiled=True),
    )
    rkv_shard, out_shard = reduce_pair(rkv_grad, out_grad)
    key_shard, value_shard = reduce_pair(key_grad, value_grad)
    return (
        block_output,
        input_grad,
        d_first,
        rkv_shard,
        out_shard,
        key_shard,
        value_shard,
        channel_shard,
        low_shard,
    )


def solution(mesh):
    return jax.shard_map(
        on_device,
        mesh=mesh,
        in_specs=(
            P("seq", None),
            P("seq", "head"),
            P("seq", None),
            P(),
            P(None, "seq", "head"),
            P("head", "seq"),
            P("head", "seq"),
            P("head", "seq"),
            P(None, "seq"),
            P(None, "seq"),
        ),
        out_specs=(
            P("seq", None),
            P("seq", None),
            P("seq", "head"),
            P(None, "seq", "head"),
            P("head", "seq"),
            P("head", "seq"),
            P("head", "seq"),
            P(None, ("seq", "head")),
            P(None, ("seq", "head")),
        ),
        check_vma=False,
    )
```

profile of v0, /device:TPU:10, one launch (start us, length us, event | category | flops | bytes accessed | tf_op | source)
XLA Modules:
  0.0 2122.4 jit_solution(2059258467816818613)
XLA Ops:
  8.7 30.7 %all-gather.4 = bf16[16,64,19]{1,2,0:T(8,128)(2,1)S(1)} all-gather(bf16[1,64,19]{1,2,0:T(8,128)(2,1)} %bitcast.774), channel_id=1, replica_groups=mesh['seq'=16,'head'=2] {'seq'}, dimensions={0}, use_global_device_ids=true | all-gather | bytes 41344 | tf_op jit(solution)/shard_map/all_gather | solution.py:472
  55.1 12.6 all-gather.17.cloned.1.call-done
  80.2 58.6 %all-gather.15.cloned.1.call-done = bf16[3,1024,512]{2,1,0:T(8,128)(2,1)} async-done(((bf16[3,64,512]{2,1,0:T(8,128)(2,1)}), bf16[3,1024,512]{2,1,0:T(8,128)(2,1)}) %all-gather.15.cloned.1.call-update) | async-done | bytes 3145744 | tf_op jit(solution)/shard_map/all_gather | solution.py:468
  154.8 5.4 bitcast_multiply_fusion.2
  164.0 158.9 %custom-call.12 = f32[4,8,1,64,64]{3,4,2,1,0:T(8,128)} custom-call(f32[4,8,1,64,64]{4,3,2,1,0:T(8,128)} %fusion.154), custom_call_target="InvertDiagBlocksLowerTriangular" | custom-call | tf_op jit(solution)/shard_map/jit(_solve_triangular)/vmap(vmap())/triangular_solve/custom-call.1 | solution.py:163
  348.2 23.6 %while.110 = (s32[]{:T(128)}, f32[8,64,64]{1,2,0:T(8,128)S(1)}, f32[8,64,64]{1,2,0:T(8,128)}, f32[4,8,64,64]{3,2,1,0:T(8,128)}, f32[4,8,64,64]{3,2,1,0:T(8,128)}, /*index=5*/s32[]{:T(128)}, s32[]{:T(128)}) while((s32[]{:T(128)}, f32[8,64,64]{1,2,0:T(8,128)S(1)}, f32[8,64,64]{1,2,0:T(8,128)}, f32[4,8,64,64]{3,2,1,0:T(8,128)}, ...), condition=%wide.region_7.9_spmd.clone, body=%wide.region_6.8_spmd.clone.sunk | while | flops 50397184 | bytes 2228331 | solution.py:327
  386.6 45.1 %all-gather.25.cloned.1.call-done = bf16[128,64,64]{2,1,0:T(8,128)(2,1)} async-done(((bf16[8,64,64]{2,1,0:T(8,128)(2,1)}), bf16[128,64,64]{2,1,0:T(8,128)(2,1)}) %all-gather.25.cloned.1.call-update) | async-done | bytes 1048592 | tf_op jit(solution)/shard_map/all_gather | solution.py:31
  431.8 62.0 %all-gather.27.cloned.1.call-done = bf16[128,64,64]{2,1,0:T(8,128)(2,1)} async-done(((bf16[8,64,64]{2,1,0:T(8,128)(2,1)}), bf16[128,64,64]{2,1,0:T(8,128)(2,1)}) %all-gather.27.cloned.1.call-update) | async-done | bytes 1048592 | tf_op jit(solution)/shard_map/all_gather | solution.py:31
  493.8 11.7 while.106
  510.1 62.5 %while.107 = (s32[]{:T(128)}, f32[8,64,64]{2,1,0:T(8,128)S(1)}, f32[4,8,64,64]{3,2,1,0:T(8,128)}, f32[4,8,64,64]{3,2,1,0:T(8,128)}, f32[4,8,64,64]{3,2,1,0:T(8,1...) while((s32[]{:T(128)}, f32[8,64,64]{2,1,0:T(8,128)S(1)}, ...), condition=%wide.region_11.13_spmd, body=%wide.region_10.12_spmd.sunk | while | flops 151322624 | bytes 6579453 | solution.py:243
  593.2 39.7 %all-reduce.6.cloned.1.call-done = bf16[256,1024]{1,0:T(8,128)(2,1)} async-done(((bf16[256,1024]{1,0:T(8,128)(2,1)}), bf16[256,1024]{1,0:T(8,128)(2,1)}) %all-reduce.6.cloned.1.call-update) | async-done | bytes 524304 | tf_op jit(solution)/shard_map/psum | solution.py:543
  642.4 70.6 %all-gather.21.cloned.1.call-done = bf16[2048,1024]{0,1:T(8,128)(2,1)} async-done(((bf16[2048,64]{0,1:T(8,128)(2,1)}), bf16[2048,1024]{0,1:T(8,128)(2,1)}) %all-gather.21.cloned.1.call-update) | async-done | bytes 4194320 | tf_op jit(solution)/shard_map/all_gather | solution.py:470
  713.0 5.0 convolution_maximum_fusion
  718.0 72.9 %all-gather.23.cloned.1.call-done = bf16[2048,1024]{0,1:T(8,128)(2,1)} async-done(((bf16[2048,64]{0,1:T(8,128)(2,1)}), bf16[2048,1024]{0,1:T(8,128)(2,1)}) %all-gather.23.cloned.1.call-update) | async-done | bytes 4194320 | tf_op jit(solution)/shard_map/all_gather | solution.py:471
  816.6 8.5 all-reduce.8.cloned.1.call-done
  842.6 27.8 %while.111 = (s32[]{:T(128)}, f32[8,64,64]{2,1,0:T(8,128)S(1)}, f32[4,8,1,64]{3,1,2,0:T(8,128)}, f32[4,8,64,64]{2,3,1,0:T(8,128)S(1)}, f32[4,8,64,64]{3,2,1,0:T(...) while((s32[]{:T(128)}, f32[8,64,64]{2,1,0:T(8,128)S(1)}, ...), condition=%wide.region_26.28_spmd.clone, body=%wide.region_25.27_spmd.clone.sunk | while | flops 100990976 | bytes 3161351 | solution.py:243
  875.6 5.0 convolution_convert_fusion.1
  889.8 62.7 %all-gather.31.cloned.1.call-done = bf16[128,64,64]{2,1,0:T(8,128)(2,1)} async-done(((bf16[8,64,64]{2,1,0:T(8,128)(2,1)}), bf16[128,64,64]{2,1,0:T(8,128)(2,1)}) %all-gather.31.cloned.1.call-update) | async-done | bytes 1048592 | tf_op jit(solution)/shard_map/all_gather | solution.py:53
  953.2 46.2 %while.108 = (s32[]{:T(128)}, f32[8,64,64]{1,2,0:T(8,128)}, s32[]{:T(128)}, bf16[16,8,64,64]{3,2,1,0:T(8,128)(2,1)}, bf16[16,8,64,64]{3,2,1,0:T(8,128)(2,1)}, /*index=5*/s32[]{:T(128)}, s32[]{:T(128)}, s32[]{:T(128)}, s32[]{:T(128)}) while((s32[]{:T(128)}, f32[8,64,64]{1,2,0:T(8,128)}, s32[]{:T(128)}, bf16[16,8,64,64]{3,2,1,0:T(8,128)(2,1)}, ...), condition=%wide.region_28.30_spmd, body=%wide.region_27.29_spmd.sunk | while | flops 25231364 | bytes 1048731 | solution.py:70
  1009.4 94.2 %while.109 = (s32[]{:T(128)}, f32[8,64,64]{2,1,0:T(8,128)S(1)}, f32[4,8,64,64]{3,2,1,0:T(8,128)}, f32[4,8,64,64]{3,2,1,0:T(8,128)}, f32[4,8,64,64]{3,2,1,0:T(8,1...) while((s32[]{:T(128)}, f32[8,64,64]{2,1,0:T(8,128)S(1)}, ...), condition=%wide.region_31.33_spmd, body=%wide.region_29.32_spmd.sunk | while | flops 302513664 | bytes 11837753 | solution.py:243
  1139.5 4.6 multiply_bitcast_fusion.3
  1199.9 7.3 collective-permute-start.3
  1238.2 4.5 concatenate.31
  1250.4 4.6 fusion.298
  1255.1 6.2 fusion.233
  1261.4 87.1 %reduce-scatter.19.cloned.1.call-done = f32[32,19]{1,0:T(8,128)} async-done(((f32[1024,19]{1,0:T(8,128)}), f32[32,19]{1,0:T(8,128)}) %reduce-scatter.19.cloned.1.call-update) | async-done | bytes 2448
  1349.8 40.9 %all-reduce.10.cloned.1.call-done = (bf16[256,1024]{1,0:T(8,128)(2,1)}, bf16[256,1024]{1,0:T(8,128)(2,1)}) async-done(((bf16[256,1024]{1,0:T(8,128)(2,1)}, bf16[256,1024]{1,0:T(8,128)(2,1)}), (bf16[256,1024]{1,0:T(8,128)(2,1)}, bf16[256,1024]{1,0:T(8,128)(2,1)})) %all-reduce.10.cloned.1.call-update) | async-done | bytes 1048592 | tf_op jit(solution)/shard_map/psum | solution.py:553
  1394.1 71.1 %reduce-scatter.11.cloned.1.call-done = f32[512,64]{0,1:T(8,128)} async-done(((f32[512,1024]{0,1:T(8,128)}), f32[512,64]{0,1:T(8,128)}) %reduce-scatter.11.cloned.1.call-update) | async-done | bytes 131088 | tf_op jit(solution)/shard_map/reduce_scatter | solution.py:450
  1465.3 122.9 %reduce-scatter.17.cloned.1.call-done = f32[576,32]{0,1:T(8,128)} async-done(((f32[576,1024]{0,1:T(8,128)}), f32[576,32]{0,1:T(8,128)}) %reduce-scatter.17.cloned.1.call-update) | async-done | bytes 73744 | tf_op jit(solution)/shard_map/reduce_scatter | solution.py:611
  1588.2 160.4 %reduce-scatter.9.cloned.1.call-done = f32[3,64,512]{2,1,0:T(8,128)} async-done(((f32[3,1024,512]{2,1,0:T(8,128)}), f32[3,64,512]{2,1,0:T(8,128)}) %reduce-scatter.9.cloned.1.call-update) | async-done | bytes 393232 | tf_op jit(solution)/shard_map/reduce_scatter | solution.py:449
  1748.5 183.7 %reduce-scatter.13.cloned.1.call-done = f32[2048,64]{0,1:T(8,128)} async-done(((f32[2048,1024]{0,1:T(8,128)}), f32[2048,64]{0,1:T(8,128)}) %reduce-scatter.13.cloned.1.call-update) | async-done | bytes 524304 | tf_op jit(solution)/shard_map/reduce_scatter | solution.py:449
  1932.2 183.0 %reduce-scatter.15.cloned.1.call-done = f32[2048,64]{0,1:T(8,128)} async-done(((f32[2048,1024]{0,1:T(8,128)}), f32[2048,64]{0,1:T(8,128)}) %reduce-scatter.15.cloned.1.call-update) | async-done | bytes 524304 | tf_op jit(solution)/shard_map/reduce_scatter | solution.py:450
  (876 shorter events, 590.0 us)
Async XLA Ops:
  7.2 60.5 %all-gather.17.cloned.1.call-start = ((), (), s32[]{:S(2)}) async-start(), calls=%async_computation.7 | async-start | bytes 1392640 | tf_op jit(solution)/shard_map/all_gather | solution.py:473
  7.9 130.9 %all-gather.15.cloned.1.call-start = ((), (), s32[]{:S(2)}) async-start(), calls=%async_computation.6 | async-start | bytes 3342336 | tf_op jit(solution)/shard_map/all_gather | solution.py:468
  8.7 423.1 %all-gather.25.cloned.1.call-start = ((), (), s32[]{:S(2)}) async-start(), calls=%async_computation.18 | async-start | bytes 2228224 | tf_op jit(solution)/shard_map/all_gather | solution.py:31
  43.1 8.7 collective-permute-start
  48.0 112.2 %copy-start.133 = (pred[64,64]{1,0:T(8,128)(4,1)}, pred[64,64]{1,0:T(8,128)(4,1)S(1)}, u32[]{:S(2)}) copy-start(pred[64,64]{1,0:T(8,128)(4,1)S(1)} %iota_compare_fusion.1) | copy-start | bytes 12292
  49.2 89.6 %copy-start.167 = (f32[1,512]{1,0:T(1,128)}, f32[1,512]{1,0:T(1,128)S(1)}, u32[]{:S(2)}) copy-start(f32[1,512]{1,0:T(1,128)S(1)} %get-tuple-element.1570) | copy-start | bytes 6148
  49.2 99.0 %copy-start.163 = (f32[1,512]{1,0:T(1,128)}, f32[1,512]{1,0:T(1,128)S(1)}, u32[]{:S(2)}) copy-start(f32[1,512]{1,0:T(1,128)S(1)} %get-tuple-element.1566) | copy-start | bytes 6148
  49.2 99.0 %copy-start.165 = (f32[1,512]{1,0:T(1,128)}, f32[1,512]{1,0:T(1,128)S(1)}, u32[]{:S(2)}) copy-start(f32[1,512]{1,0:T(1,128)S(1)} %get-tuple-element.1563) | copy-start | bytes 6148
  49.3 283.9 %copy-start.112 = (f32[64,64]{1,0:T(8,128)}, f32[64,64]{1,0:T(8,128)S(1)}, u32[]{:S(2)}) copy-start(f32[64,64]{1,0:T(8,128)S(1)} %broadcast_select_fusion) | copy-start | bytes 49156
  49.4 292.4 %copy-start.175 = (f32[4]{0:T(128)}, f32[4]{0:T(128)S(1)}, u32[]{:S(2)}) copy-start(f32[4]{0:T(128)S(1)} %subtract_reduce_fusion) | copy-start | bytes 52
  55.1 273.2 %copy-start.25 = (bf16[256,1024]{1,0:T(8,128)(2,1)}, bf16[256,1024]{1,0:T(8,128)(2,1)S(1)}, u32[]{:S(2)}) copy-start(bf16[256,1024]{1,0:T(8,128)(2,1)S(1)} %get-tuple-element.1527) | copy-start | bytes 1572868
  164.0 164.3 %copy-start.110 = (bf16[256,512]{1,0:T(8,128)(2,1)S(1)}, bf16[256,512]{1,0:T(8,128)(2,1)}, u32[]{:S(2)}) copy-start(bf16[256,512]{1,0:T(8,128)(2,1)} %param.27) | copy-start | bytes 786436
  372.6 121.2 %all-gather.27.cloned.1.call-start = ((), (), s32[]{:S(2)}) async-start(), calls=%async_computation.19 | async-start | bytes 2228224 | tf_op jit(solution)/shard_map/all_gather | solution.py:31
  374.3 214.6 %all-gather.19.cloned.1.call-start = ((), (), s32[]{:S(2)}) async-start(), calls=%async_computation.8 | async-start | bytes 1114112 | tf_op jit(solution)/shard_map/all_gather | solution.py:469
  374.9 257.9 %all-reduce.6.cloned.1.call-start = ((), (), s32[]{:S(2)}) async-start(), calls=%async_computation.9 | async-start | bytes 1048576 | tf_op jit(solution)/shard_map/psum | solution.py:543
  376.6 506.9 %copy-start.109 = (f32[256,128]{1,0:T(8,128)}, f32[256,128]{1,0:T(8,128)S(1)}, u32[]{:S(2)}) copy-start(f32[256,128]{1,0:T(8,128)S(1)} %fusion.174) | copy-start | bytes 393220
  591.6 121.4 %all-gather.21.cloned.1.call-start = ((), (), s32[]{:S(2)}) async-start(), calls=%async_computation.10 | async-start | bytes 4456448 | tf_op jit(solution)/shard_map/all_gather | solution.py:470
  592.3 198.5 %all-gather.23.cloned.1.call-start = ((), (), s32[]{:S(2)}) async-start(), calls=%async_computation.11 | async-start | bytes 4456448 | tf_op jit(solution)/shard_map/all_gather | solution.py:471
  593.1 232.0 %all-reduce.8.cloned.1.call-start = ((), (), s32[]{:S(2)}) async-start(), calls=%async_computation.12 | async-start | bytes 1048576 | tf_op jit(solution)/shard_map/psum | solution.py:568
  635.9 5.5 collective-permute-start.1
  797.4 6.4 collective-permute-start.2
  806.4 83.4 %all-gather.29.cloned.1.call-start = ((), (), s32[]{:S(2)}) async-start(), calls=%async_computation.20 | async-start | bytes 2228224 | tf_op jit(solution)/shard_map/all_gather | solution.py:53
  812.1 140.4 %all-gather.31.cloned.1.call-start = ((), (), s32[]{:S(2)}) async-start(), calls=%async_computation.21 | async-start | bytes 2228224 | tf_op jit(solution)/shard_map/all_gather | solution.py:53
  871.1 477.4 %reduce-scatter.19.cloned.1.call-start = ((), (), s32[]{:S(2)}) async-start(), calls=%async_computation.22 | async-start | bytes 540672
  1199.9 12.5 collective-permute-start.3
  1222.8 167.9 %all-reduce.10.cloned.1.call-start = ((), (), s32[]{:S(2)}) async-start(), calls=%async_computation.23 | async-start | bytes 2097152 | tf_op jit(solution)/shard_map/psum | solution.py:553
  1223.8 241.5 %reduce-scatter.11.cloned.1.call-start = ((), (), s32[]{:S(2)}) async-start(), calls=%async_computation.14 | async-start | bytes 2228224 | tf_op jit(solution)/shard_map/reduce_scatter | solution.py:450
  1226.7 361.5 %reduce-scatter.17.cloned.1.call-start = ((), (), s32[]{:S(2)}) async-start(), calls=%async_computation.17 | async-start | bytes 2703360 | tf_op jit(solution)/shard_map/reduce_scatter | solution.py:611
  1242.8 505.8 %reduce-scatter.9.cloned.1.call-start = ((), (), s32[]{:S(2)}) async-start(), calls=%async_computation.13 | async-start | bytes 6684672 | tf_op jit(solution)/shard_map/reduce_scatter | solution.py:449
  1249.1 683.1 %reduce-scatter.13.cloned.1.call-start = ((), (), s32[]{:S(2)}) async-start(), calls=%async_computation.15 | async-start | bytes 8912896 | tf_op jit(solution)/shard_map/reduce_scatter | solution.py:449
  1255.1 860.1 %reduce-scatter.15.cloned.1.call-start = ((), (), s32[]{:S(2)}) async-start(), calls=%async_computation.16 | async-start | bytes 8912896 | tf_op jit(solution)/shard_map/reduce_scatter | solution.py:450
  1261.3 131.6 %copy-start.65 = (bf16[256,1024]{1,0:T(8,128)(2,1)S(1)}, bf16[256,1024]{1,0:T(8,128)(2,1)}, u32[]{:S(2)}) copy-start(bf16[256,1024]{1,0:T(8,128)(2,1)} %all-reduce.8.cloned.1.call-done) | copy-start | bytes 1572868
  (178 other events, 1166.1 us)
Sparse Core Ops, SparseCore 0:
  10.8 56.8 all-gather.16
  70.4 68.3 all-gather.14
  372.7 59.0 all-gather.24
  434.4 59.3 all-gather.26
  496.4 53.0 all-gather.18
  591.7 41.0 all-reduce.5
  636.0 76.9 all-gather.20
  716.1 74.6 all-gather.22
  806.5 18.5 all-reduce.7
  828.3 61.4 all-gather.28
  893.1 59.3 all-gather.30
  1222.9 125.4 reduce-scatter.18
  1350.9 39.7 all-reduce.9
  1393.4 71.7 reduce-scatter.10
  1468.0 120.1 reduce-scatter.16
  1590.9 157.5 reduce-scatter.8
  1751.2 180.9 reduce-scatter.12
  1934.9 180.2 reduce-scatter.14
where the time goes:
time: 2140 us; the launch traced here: 2120 us
  waiting for transfers between devices  1300 us (61%)
  matrix products  338 us (16%)
  other arithmetic  230 us (11%)
  local copies, waits for them, and re-layouts  189 us (9%)
  blocking collectives  30.7 us (1%)
    reduce_scatter x2, waiting for transfers between devices, reduce_pair(): lax.psum_scatter(first_grad, 'seq', scatter_dimension=1, tiled=True)  344 us
    reduce_scatter x2, waiting for transfers between devices, reduce_pair(): lax.psum_scatter(second_grad, 'seq', scatter_dimension=1, tiled=True)  254 us
    another operation x4, other arithmetic, span_parts(): jax.scipy.linalg.solve_triangular(system, unit_back, lower=True, unit_dia...  159 us
    reduce_scatter x1, waiting for transfers between devices, on_device(): lax.psum_scatter(low_rank_grad, ('seq', 'head'), scatter_dimension=1, til...  123 us
    all_gather x2, waiting for transfers between devices, prefix(): lax.all_gather(a.astype(kind), axis)  107 us
    unnamed x19, waiting for transfers between devices  90.6 us
    all_gather x1, waiting for transfers between devices, on_device(): lax.all_gather(ffn_value, 'seq', axis=1, tiled=True)  72.9 us
    all_gather x1, waiting for transfers between devices, on_device(): lax.all_gather(ffn_key, 'seq', axis=1, tiled=True)  70.6 us
  transfers between devices with their start and end apart: 22, of which 20 were waited for; matrix products, arithmetic and copies ran while one was open for 12% of the time, Pallas kernels for 0%

commit v1 on v0

v1 whole, which is shorter than its diff:
```python
from functools import partial

import jax
import jax.numpy as jnp
from jax import lax
from jax.experimental import pallas as pl
from jax.experimental.pallas import tpu as pltpu
from jax.sharding import PartitionSpec as P

HEAD_SIZE = 64
DECAY_RANK = 64
RATE_RANK = 64
VALUE_RANK = 32
RANKS = 288
SPAN = 64


norm_eps = 1e-05
group_eps = 0.00064
key_eps = 1e-06
highest = lax.Precision.HIGHEST


def shifted(array, axis, by):
    size = lax.axis_size(axis)
    pairs = [(i, i + by) for i in range(size) if 0 <= i + by < size]
    return lax.ppermute(array, axis, pairs)


def dot_plain(left, right):
    return jnp.dot(left, right, preferred_element_type=jnp.float32)


def dot_rows(left, right):
    return lax.dot_general(
        left, right, (((1,), (1,)), ((), ())), preferred_element_type=jnp.float32
    )


def dot_tokens(left, right):
    return lax.dot_general(
        left, right, (((0,), (0,)), ((), ())), preferred_element_type=jnp.float32
    )


def dot_high(left, right):
    return jnp.dot(left, right, precision=highest, preferred_element_type=jnp.float32)


def tokens_high(left, right):
    return lax.dot_general(
        left, right, (((0,), (0,)), ((), ())), precision=highest, preferred_element_type=jnp.float32
    )


def layer_norm(inputs, gain, bias):
    centre = inputs - jnp.mean(inputs, axis=-1, keepdims=True)
    spread = jnp.mean(centre * centre, axis=-1, keepdims=True)
    return centre * lax.rsqrt(spread + norm_eps) * gain + bias


def raw_dot(left, right, kind):
    dims = {"nn": ((1,), (0,)), "nt": ((1,), (1,)), "tn": ((0,), (0,))}[kind]
    return lax.dot_general(
        left, right, (dims, ((), ())), precision=highest, preferred_element_type=jnp.float32
    )


@partial(jax.custom_vjp, nondiff_argnums=(2,))
def mul(left, right, kind):
    return raw_dot(left, right, kind)


def mul_fwd(left, right, kind):
    return raw_dot(left, right, kind), (left, right)


def mul_bwd(kind, saved, grad):
    left, right = saved
    if kind == "nn":
        return raw_dot(grad, right, "nt"), raw_dot(left, grad, "tn")
    if kind == "nt":
        return raw_dot(grad, right, "nn"), raw_dot(grad, left, "tn")
    return raw_dot(right, grad, "nt"), raw_dot(left, grad, "nn")


mul.defvjp(mul_fwd, mul_bwd)


@jax.custom_vjp
def solved(lower, right, inverse):
    return raw_dot(inverse, right, "nn")


def solved_fwd(lower, right, inverse):
    out = raw_dot(inverse, right, "nn")
    return out, (inverse, out)


def solved_bwd(saved, grad):
    inverse, out = saved
    right_grad = raw_dot(inverse, grad, "tn")
    return -raw_dot(right_grad, out, "nt"), right_grad, jnp.zeros_like(inverse)


solved.defvjp(solved_fwd, solved_bwd)


def grid_masks():
    row = lax.broadcasted_iota(jnp.int32, (SPAN, SPAN), 0)
    column = lax.broadcasted_iota(jnp.int32, (SPAN, SPAN), 1)
    return row, column


def inverse_of(lowers):
    row, column = grid_masks()
    eye = (row == column).astype(jnp.float32)
    outs = None
    size = 1
    while size < SPAN:
        shift = size.bit_length() - 1
        rb, cb = row >> shift, column >> shift
        mask = ((rb >> 1) == (cb >> 1)) & (rb > cb)
        parts = [jnp.where(mask, lower, 0.0) for lower in lowers]
        if outs is None:
            outs = [eye - part for part in parts]
        else:
            halves = [raw_dot(out, part, "nn") for out, part in zip(outs, parts)]
            outs = [out - raw_dot(half, out, "nn") for out, half in zip(outs, halves)]
        size *= 2
    return outs


def prepare(key_raw, value_raw, first, decay_pre, rate_pre, mix_pre, key_scale, rate_scale):
    log_decay = -jnp.exp(-jax.nn.softplus(-decay_pre) - 0.5)
    in_rate = jax.nn.sigmoid(rate_pre)
    value_new = value_raw + (first - value_raw) * jax.nn.sigmoid(mix_pre)
    scaled = key_raw * key_scale
    key_unit = scaled * lax.rsqrt(jnp.sum(scaled * scaled, axis=-1, keepdims=True) + key_eps)
    key_taken = key_unit * in_rate
    key_final = key_raw * (1.0 + (in_rate - 1.0) * rate_scale)
    return log_decay, key_unit, key_taken, value_new, key_final


@jax.custom_vjp
def quarters(whole):
    half = whole.shape[0] // 2
    return whole[:half, :half], whole[:half, half:], whole[half:, :half], whole[half:, half:]


def quarters_fwd(whole):
    return quarters(whole), None


def quarters_bwd(_, grads):
    upper = jnp.concatenate([grads[0], grads[1]], axis=1)
    lower = jnp.concatenate([grads[2], grads[3]], axis=1)
    return (jnp.concatenate([upper, lower], axis=0),)


quarters.defvjp(quarters_fwd, quarters_bwd)


def span_start(recept, log_decay, key_unit, key_taken, key_final):
    row, column = grid_masks()
    inclusive = (row >= column).astype(jnp.float32)
    log_total = mul(inclusive, log_decay, "nn")
    gamma = jnp.exp(log_total)
    before = jnp.exp(log_total - log_decay)
    inverse = jnp.exp(-log_total)
    unit_back = key_unit * before
    key_hat = key_final * inverse
    taken_hat = key_taken * inverse
    strict = (row > column).astype(jnp.float32)
    upper = jnp.concatenate([strict, strict], axis=1)
    under = jnp.concatenate([inclusive, inclusive], axis=1)
    asking = jnp.concatenate([unit_back, recept * gamma], axis=0)
    asked_of = jnp.concatenate([key_hat, taken_hat], axis=0)
    scores = mul(asking, asked_of, "nt") * jnp.concatenate([upper, under], axis=0)
    cross_key, lower, read_key, read_taken = quarters(scores)
    end = jnp.exp(jnp.sum(log_decay, axis=0, keepdims=True))
    return gamma, unit_back, key_hat, taken_hat, lower, cross_key, read_key, read_taken, end


def span_end(recept, value_new, start, inverse):
    gamma, unit_back, key_hat, taken_hat, lower, cross_key, read_key, read_taken, end = start
    row, column = grid_masks()
    carried = solved(lower, unit_back, inverse)
    base = solved(lower, mul(cross_key, value_new, "nn"), inverse)
    tilde = recept * gamma
    asked = tilde - mul(read_taken, carried, "nn")
    own = mul(read_key, value_new, "nn") - mul(read_taken, base, "nn")
    eye = (row == column).astype(jnp.float32)
    matrix = (eye - mul(carried, taken_hat, "tn")) * end
    offset_state = (mul(value_new, key_hat, "tn") - mul(base, taken_hat, "tn")) * end
    return asked, own, matrix, offset_state


def output_of(read, recept, key_final, value_new, gate, bonus, gain, bias):
    centre = read - jnp.mean(read, axis=-1, keepdims=True)
    spread = jnp.mean(centre * centre, axis=-1, keepdims=True)
    normed = centre * lax.rsqrt(spread + group_eps) * gain + bias
    extra = jnp.sum(recept * key_final * bonus, axis=-1, keepdims=True) * value_new
    return (normed + extra) * gate


def heads_of(ref):
    lanes = ref.shape[-1] // HEAD_SIZE
    whole = ref[...].astype(jnp.float32)
    return [whole[:, i * HEAD_SIZE : (i + 1) * HEAD_SIZE] for i in range(lanes)]


def parts_kernel(r, k, v, f, d, a, m, rows, inverse_out, maps_out, asked_out, own_out):
    tokens = list(zip(*[heads_of(x) for x in (r, k, v, f, d, a, m)]))
    params = heads_of(rows)
    ready = [prepare(*t[1:], p[0:1], p[1:2]) for t, p in zip(tokens, params)]
    starts = [span_start(t[0], x[0], x[1], x[2], x[4]) for t, x in zip(tokens, ready)]
    inverses = inverse_of([s[4] for s in starts])
    asks, owns = [], []
    for i, (t, x, s, inv) in enumerate(zip(tokens, ready, starts, inverses)):
        asked, own, matrix, offset_state = span_end(t[0], x[3], s, inv)
        inverse_out[0, i] = inv
        maps_out[0, i, 0:HEAD_SIZE, :] = matrix
        maps_out[0, i, HEAD_SIZE : 2 * HEAD_SIZE, :] = offset_state
        asks.append(asked)
        owns.append(own)
    asked_out[...] = jnp.concatenate(asks, axis=1)
    own_out[...] = jnp.concatenate(owns, axis=1)


def finish(recept, key_raw, value_raw, first, rate_pre, mix_pre, gate, p, read):
    zero = jnp.zeros_like(rate_pre)
    _, _, _, value_new, key_final = prepare(
        key_raw, value_raw, first, zero, rate_pre, mix_pre, p[0:1], p[1:2]
    )
    return output_of(read, recept, key_final, value_new, gate, p[2:3], p[3:4], p[4:5])


def output_kernel(r, k, v, f, a, m, g, rows, asked, own, state, out):
    outs = []
    tokens = zip(*[heads_of(x) for x in (r, k, v, f, a, m, g, rows, asked, own)])
    for i, t in enumerate(tokens):
        read = t[9] + raw_dot(t[8], state[0, i], "nt")
        outs.append(finish(*t[:8], read))
    out[...] = jnp.concatenate(outs, axis=1).astype(out.dtype)


def state_back_kernel(r, k, v, f, a, m, g, rows, asked, own, state, cot, state_grad):
    tokens = zip(*[heads_of(x) for x in (r, k, v, f, a, m, g, rows, asked, own, cot)])
    for i, t in enumerate(tokens):
        read = t[9] + raw_dot(t[8], state[0, i], "nt")
        _, back = jax.vjp(partial(finish, *t[:8]), read)
        state_grad[0, i] = raw_dot(back(t[10])[0], t[8], "tn")


def whole_span(inverse, state, recept, key_raw, value_raw, first, decay_pre, rate_pre, mix_pre, gate, *p):
    log_decay, key_unit, key_taken, value_new, key_final = prepare(
        key_raw, value_raw, first, decay_pre, rate_pre, mix_pre, p[0], p[1]
    )
    start = span_start(recept, log_decay, key_unit, key_taken, key_final)
    asked, own, matrix, offset_state = span_end(recept, value_new, start, inverse)
    read = own + mul(asked, state, "nt")
    out = output_of(read, recept, key_final, value_new, gate, p[2], p[3], p[4])
    return out, mul(state, matrix, "nn") + offset_state


def back_kernel(r, k, v, f, d, a, m, g, rows, inverse, state, cot, next_grad, *outs):
    tokens = zip(*[heads_of(x) for x in (r, k, v, f, d, a, m, g, rows, cot)])
    columns = []
    for i, t in enumerate(tokens):
        p = tuple(t[8][j : j + 1] for j in range(5))
        _, back = jax.vjp(partial(whole_span, inverse[0, i], state[0, i]), *t[:8], *p)
        columns.append(back((t[9], next_grad[0, i])))
    for j in range(8):
        outs[j][...] = jnp.concatenate([c[j] for c in columns], axis=1).astype(outs[j].dtype)
    for j in range(5):
        outs[8][0, j : j + 1, :] = jnp.concatenate([c[8 + j] for c in columns], axis=1)
    outs[8][0, 5:8, :] = jnp.zeros((3, outs[8].shape[2]), jnp.float32)


LANES = 128
PAIR = LANES // HEAD_SIZE
token_spec = pl.BlockSpec((SPAN, LANES), lambda z, h: (z, h))
rows_spec = pl.BlockSpec((8, LANES), lambda z, h: (0, h))
square_spec = pl.BlockSpec((1, PAIR, HEAD_SIZE, HEAD_SIZE), lambda z, h: (z, h, 0, 0))
maps_spec = pl.BlockSpec((1, PAIR, 2 * HEAD_SIZE, HEAD_SIZE), lambda z, h: (z, h, 0, 0))
sums_spec = pl.BlockSpec((1, 8, LANES), lambda z, h: (z, 0, h))


def run(kernel, arrays, in_specs, out_specs, out_shapes, flops):
    tokens, width = arrays[0].shape
    moved = sum(a.size * a.dtype.itemsize for a in arrays)
    return pl.pallas_call(
        kernel,
        grid=(tokens // SPAN, width // LANES),
        in_specs=in_specs,
        out_specs=out_specs,
        out_shape=out_shapes,
        compiler_params=pltpu.CompilerParams(vmem_limit_bytes=32 * 1024 * 1024),
        cost_estimate=pl.CostEstimate(flops=flops, bytes_accessed=2 * moved, transcendentals=0),
    )(*arrays)


def joined(earlier, later):
    size = later.shape[-1]
    return jnp.einsum("...ij,...jk->...ik", earlier, later[..., :size, :], precision=highest) + jnp.concatenate(
        [jnp.zeros_like(later[..., :size, :]), later[..., size:, :]], axis=-2
    )


def before(own, place):
    count = lax.axis_size("seq")
    size = own.shape[-1]
    eye = jnp.broadcast_to(jnp.eye(size, dtype=own.dtype), own[:, :size].shape)
    total, ahead = own, jnp.concatenate([eye, jnp.zeros_like(eye)], axis=1)
    step = 1
    while step < count:
        pairs = [(i, i ^ step) for i in range(count)]
        other = lax.ppermute(total.astype(jnp.bfloat16), "seq", pairs).astype(jnp.float32)
        upper = (place & step) != 0
        ahead = jnp.where(upper, joined(other, ahead), ahead)
        if 2 * step < count:
            total = joined(jnp.where(upper, other, total), jnp.where(upper, total, other))
        step *= 2
    return ahead[:, size:]


def head_sum(part):
    own = part.astype(jnp.bfloat16)
    pairs = [(i, i ^ 1) for i in range(lax.axis_size("head"))]
    other = lax.ppermute(own, "head", pairs)
    return own.astype(jnp.float32) + other.astype(jnp.float32)


def gathered(shard):
    return lax.all_gather(shard, "seq", axis=0, tiled=True)


def scattered(full):
    return lax.psum_scatter(
        full.astype(jnp.bfloat16), "seq", scatter_dimension=0, tiled=True
    ).astype(jnp.float32)

def project(mixed_rows, rkv_cols, maps_in, maps_out, chan_params):
    first_end = DECAY_RANK
    second_end = first_end + RATE_RANK
    third_end = second_end + VALUE_RANK
    query_vector_lines = dot_plain(mixed_rows[0], rkv_cols[0])
    lookup_vector_mapped = dot_plain(mixed_rows[2], rkv_cols[1])
    payload_vector_mapped = dot_plain(mixed_rows[3], rkv_cols[2])
    decay_hidden = jnp.tanh(dot_plain(mixed_rows[1], maps_in[:, :first_end]))
    decay_low = decay_hidden.astype(jnp.bfloat16)
    forgetting_preactivation = chan_params[11] + dot_rows(decay_low, maps_out[:, :first_end])
    rate_low = dot_plain(mixed_rows[4], maps_in[:, first_end:second_end]).astype(jnp.bfloat16)
    learning_speed_preactivation = chan_params[12] + dot_rows(
        rate_low, maps_out[:, first_end:second_end]
    )
    mix_low = dot_plain(mixed_rows[3], maps_in[:, second_end:third_end]).astype(jnp.bfloat16)
    interpolation_preactivation = chan_params[13] + dot_rows(
        mix_low, maps_out[:, second_end:third_end]
    )
    gate_hidden = jax.nn.sigmoid(dot_plain(mixed_rows[5], maps_in[:, third_end:]))
    gate_low = gate_hidden.astype(jnp.bfloat16)
    emission_sigmoid_multiplier = dot_rows(gate_low, maps_out[:, third_end:])
    saved = (decay_hidden, decay_low, rate_low, mix_low, gate_hidden, gate_low)
    return (
        saved,
        (
            query_vector_lines,
            lookup_vector_mapped,
            payload_vector_mapped,
            forgetting_preactivation,
            learning_speed_preactivation,
            interpolation_preactivation,
            emission_sigmoid_multiplier,
        ),
    )


def rank_dot(ranks, maps_in):
    high = ranks.astype(jnp.bfloat16)
    low = (ranks - high.astype(jnp.float32)).astype(jnp.bfloat16)
    return dot_rows(high, maps_in) + dot_rows(low, maps_in)


def rank_tokens(rows, ranks):
    high = ranks.astype(jnp.bfloat16)
    low = (ranks - high.astype(jnp.float32)).astype(jnp.bfloat16)
    return dot_tokens(rows, high) + dot_tokens(rows, low)


def project_back(mixed_rows, rkv_cols, maps_in, maps_out, saved, grads_in):
    first_end = DECAY_RANK
    second_end = first_end + RATE_RANK
    third_end = second_end + VALUE_RANK
    decay_hidden, decay_low, rate_low, mix_low, gate_hidden, gate_low = saved
    recept_low, key_low, value_low, decay_back, rate_back, mix_back_low, gate_back = grads_in
    rkv_grad = [
        dot_tokens(mixed_rows[0], recept_low),
        dot_tokens(mixed_rows[2], key_low),
        dot_tokens(mixed_rows[3], value_low),
    ]
    decay_rank = dot_plain(decay_back, maps_out[:, :first_end]) * (
        1.0 - decay_hidden * decay_hidden
    )
    rate_rank = dot_plain(rate_back, maps_out[:, first_end:second_end])
    mix_rank = dot_plain(mix_back_low, maps_out[:, second_end:third_end])
    gate_rank = dot_plain(gate_back, maps_out[:, third_end:]) * gate_hidden * (1.0 - gate_hidden)
    out_grads = jnp.concatenate(
        [
            dot_tokens(decay_back, decay_low),
            dot_tokens(rate_back, rate_low),
            dot_tokens(mix_back_low, mix_low),
            dot_tokens(gate_back, gate_low),
        ],
        axis=1,
    )
    in_grads = jnp.concatenate(
        [
            rank_tokens(mixed_rows[1], decay_rank),
            rank_tokens(mixed_rows[4], rate_rank),
            rank_tokens(mixed_rows[3], mix_rank),
            rank_tokens(mixed_rows[5], gate_rank),
        ],
        axis=1,
    )
    grad_recept = dot_rows(recept_low, rkv_cols[0])
    grad_decay = rank_dot(decay_rank, maps_in[:, :first_end])
    grad_key = dot_rows(key_low, rkv_cols[1])
    grad_value = dot_rows(value_low, rkv_cols[2]) + rank_dot(
        mix_rank, maps_in[:, second_end:third_end]
    )
    grad_rate = rank_dot(rate_rank, maps_in[:, first_end:second_end])
    grad_gate = rank_dot(gate_rank, maps_in[:, third_end:])
    return (
        [grad_recept, grad_decay, grad_key, grad_value, grad_rate, grad_gate],
        rkv_grad,
        in_grads,
        out_grads,
    )


def shift_diff(standardized_layer_entry, edge_row, keep_mask):
    previous = jnp.concatenate([edge_row, standardized_layer_entry[:-1]], axis=0) * keep_mask
    return previous - standardized_layer_entry


def mix_back(grads_list, coeffs, shifted_diff, keep_mask):
    direct = jnp.zeros_like(shifted_diff)
    carried = jnp.zeros_like(shifted_diff)
    for column, grad_rows in enumerate(grads_list):
        direct = direct + grad_rows * (1.0 - coeffs[column])
        carried = carried + grad_rows * coeffs[column]
    coeff_grads = jnp.stack([jnp.sum(grad_rows * shifted_diff, axis=0) for grad_rows in grads_list])
    return (direct, carried * keep_mask, coeff_grads)


def on_device(
    block_input,
    value_first,
    out_cotangent,
    seq_lengths,
    w_rkv,
    w_out,
    ffn_key,
    ffn_value,
    channel_params,
    low_rank,
):
    tokens_dev, width = block_input.shape
    local_width = w_rkv.shape[2]
    spans = tokens_dev // SPAN
    heads_dev = local_width // HEAD_SIZE
    place = lax.axis_index("seq")
    offset = lax.axis_index("head") * local_width
    small = jnp.concatenate([low_rank, channel_params], axis=0)
    small_rows = small.shape[0]
    packed = -(-small_rows // 128) * 128
    small_all = gathered(jnp.pad(small, ((0, packed - small_rows), (0, 0))).T)
    rkv_all = lax.all_gather(w_rkv, "seq", axis=1, tiled=True)
    out_all = gathered(w_out.T)
    key_all = gathered(ffn_key.T)
    value_all = gathered(ffn_value.T)
    params = small_all[:, 2 * RANKS : small_rows].astype(jnp.float32).T
    local_params = lax.dynamic_slice_in_dim(params, offset, local_width, 1)
    maps_in = small_all[:, :RANKS]
    maps_out = lax.dynamic_slice_in_dim(small_all[:, RANKS : 2 * RANKS], offset, local_width, 0)
    position = place * tokens_dev + jnp.arange(tokens_dev, dtype=jnp.int32)
    order = jnp.arange(seq_lengths.shape[0])
    earlier = jnp.where(order[None, :] < order[:, None], seq_lengths[None, :], 0)
    starts = jnp.sum(earlier, axis=1) * SPAN
    resets = jnp.any(position[:, None] == starts[None, :], axis=1).astype(jnp.float32)
    keep_mask = (1.0 - resets)[:, None]
    keep_span = (1.0 - resets.reshape(spans, SPAN)[:, 0])[:, None, None, None]
    inputs_float = block_input.astype(jnp.float32)
    normed_one = layer_norm(inputs_float, params[0], params[1])
    edge_one = shifted(normed_one[-1:], "seq", 1)
    diff_one = shift_diff(normed_one, edge_one, keep_mask)
    mixed_rows = [
        (normed_one + diff_one * params[4 + column]).astype(jnp.bfloat16) for column in range(6)
    ]
    saved, mixer_args = project(mixed_rows, rkv_all, maps_in, maps_out, local_params)
    recept, key_raw, value_raw, decay_pre, rate_pre, mix_pre, gate = mixer_args
    rows = jnp.pad(local_params[14:19], ((0, 3), (0, 0)))
    wide = jax.ShapeDtypeStruct((tokens_dev, local_width), jnp.float32)
    wide_low = jax.ShapeDtypeStruct((tokens_dev, local_width), jnp.bfloat16)
    square = jax.ShapeDtypeStruct((spans, heads_dev, HEAD_SIZE, HEAD_SIZE), jnp.float32)
    double = jax.ShapeDtypeStruct((spans, heads_dev, 2 * HEAD_SIZE, HEAD_SIZE), jnp.float32)
    sums = jax.ShapeDtypeStruct((spans, 8, local_width), jnp.float32)
    inverse, maps, asked, own = run(
        parts_kernel,
        (recept, key_raw, value_raw, value_first, decay_pre, rate_pre, mix_pre, rows),
        [token_spec] * 7 + [rows_spec],
        [square_spec, maps_spec, token_spec, token_spec],
        [square, double, wide, wide],
        2 * 10**9,
    )
    span_mats = maps[:, :, :HEAD_SIZE] * keep_span
    maps = jnp.concatenate([span_mats, maps[:, :, HEAD_SIZE:]], axis=2)
    upto = [maps[0]]
    for z in range(1, spans):
        upto.append(joined(upto[-1], maps[z]))
    state_first = before(upto[-1], place)
    states = jnp.stack(
        [state_first]
        + [
            jnp.einsum("hij,hjk->hik", state_first, m[:, :HEAD_SIZE], precision=highest)
            + m[:, HEAD_SIZE:]
            for m in upto[:-1]
        ]
    ) * keep_span
    mixer_low = run(
        output_kernel,
        (recept, key_raw, value_raw, value_first, rate_pre, mix_pre, gate, rows, asked, own, states),
        [token_spec] * 7 + [rows_spec] + [token_spec] * 2 + [square_spec],
        token_spec,
        wide_low,
        10**8,
    )
    residual_one = inputs_float + head_sum(dot_rows(mixer_low, out_all))
    normed_two = layer_norm(residual_one, params[2], params[3])
    edge_two = shifted(normed_two[-1:], "seq", 1)
    diff_two = shift_diff(normed_two, edge_two, keep_mask)
    mixed_ffn = (normed_two + diff_two * params[10]).astype(jnp.bfloat16)
    hidden_pre = dot_plain(mixed_ffn, key_all)
    hidden_low = jnp.square(jax.nn.relu(hidden_pre)).astype(jnp.bfloat16)
    ffn_out = head_sum(dot_rows(hidden_low, value_all))
    block_output = (residual_one + ffn_out).astype(jnp.bfloat16)
    cot_float = out_cotangent.astype(jnp.float32)
    value_shard = scattered(dot_tokens(out_cotangent, hidden_low))
    hidden_grad = dot_plain(out_cotangent, value_all)
    pre_low = (hidden_grad * 2.0 * jax.nn.relu(hidden_pre)).astype(jnp.bfloat16)
    key_shard = scattered(dot_tokens(mixed_ffn, pre_low))
    ffn_in_grad = dot_rows(pre_low, key_all)
    direct_two, carried_two, coeff_two = mix_back([ffn_in_grad], params[10:11], diff_two, keep_mask)
    from_next_two = shifted(carried_two[:1], "seq", -1)
    normed_two_grad = direct_two + jnp.concatenate([carried_two[1:], from_next_two], axis=0)
    _, norm_two_back = jax.vjp(layer_norm, residual_one, params[2], params[3])
    resid_part, gain_two, bias_two = norm_two_back(normed_two_grad)
    residual_grad = cot_float + head_sum(resid_part)
    attend_low = residual_grad.astype(jnp.bfloat16)
    out_shard = scattered(dot_tokens(attend_low, mixer_low))
    mixer_grad = dot_plain(attend_low, out_all)
    read_grads = run(
        state_back_kernel,
        (recept, key_raw, value_raw, value_first, rate_pre, mix_pre, gate, rows, asked, own, states, mixer_grad),
        [token_spec] * 7 + [rows_spec] + [token_spec] * 2 + [square_spec, token_spec],
        square_spec,
        square,
        10**8,
    ) * keep_span
    grads, tails = [None] * spans, [None] * spans
    grad_first = read_grads[spans - 1]
    tail = span_mats[spans - 1]
    tails[spans - 2] = tail
    grads[spans - 2] = grad_first
    for z in range(spans - 2, -1, -1):
        grad_first = read_grads[z] + jnp.einsum(
            "hij,hkj->hik", grad_first, span_mats[z], precision=highest
        )
        tail = jnp.einsum("hij,hjk->hik", span_mats[z], tail, precision=highest)
        if z > 0:
            grads[z - 1], tails[z - 1] = grad_first, tail
    count = lax.axis_size("seq")
    state_grad = before(
        jnp.concatenate([jnp.swapaxes(tail, 1, 2), grad_first], axis=1), count - 1 - place
    )
    next_grads = jnp.stack(
        [
            g + jnp.einsum("hij,hkj->hik", state_grad, t, precision=highest)
            for g, t in zip(grads[:-1], tails[:-1])
        ]
        + [state_grad]
    )
    next_grads, value_shard = lax.optimization_barrier((next_grads, value_shard))
    back = run(
        back_kernel,
        (recept, key_raw, value_raw, value_first, decay_pre, rate_pre, mix_pre, gate, rows, inverse, states, mixer_grad, next_grads),
        [token_spec] * 8 + [rows_spec] + [square_spec] * 2 + [token_spec, square_spec],
        [token_spec] * 8 + [sums_spec],
        [wide_low, wide_low, wide_low, wide, wide, wide, wide, wide_low, sums],
        4 * 10**9,
    )
    d_recept, d_key, d_value, d_first, d_decay, d_rate, d_mix, d_gate, param_sums = back
    bias_grads = jnp.stack(
        [jnp.sum(d_decay, axis=0), jnp.sum(d_rate, axis=0), jnp.sum(d_mix, axis=0)]
    )
    lows = [x.astype(jnp.bfloat16) for x in (d_recept, d_key, d_value, d_decay, d_rate, d_mix, d_gate)]
    mixed_grads, rkv_grad, in_grads, out_grads = project_back(
        mixed_rows, rkv_all, maps_in, maps_out, saved, lows
    )
    mixed_grads, rkv_grad, key_shard, out_shard = lax.optimization_barrier(
        (mixed_grads, rkv_grad, key_shard, out_shard)
    )
    direct_one, carried_one, coeff_one = mix_back(mixed_grads, params[4:10], diff_one, keep_mask)
    from_next_one = shifted(carried_one[:1], "seq", -1)
    normed_one_grad = direct_one + jnp.concatenate([carried_one[1:], from_next_one], axis=0)
    _, norm_one_back = jax.vjp(layer_norm, inputs_float, params[0], params[1])
    input_part, gain_one, bias_one = norm_one_back(normed_one_grad)
    input_grad = residual_grad + head_sum(input_part)
    full_rows = jnp.concatenate(
        [jnp.stack([gain_one, bias_one, gain_two, bias_two]), coeff_one, coeff_two], axis=0
    )
    head_rows = jnp.concatenate([bias_grads, jnp.sum(param_sums, axis=0)[:5]], axis=0)
    placed = lax.dynamic_update_slice_in_dim(
        jnp.zeros((width, out_grads.shape[1] + head_rows.shape[0]), jnp.float32),
        jnp.concatenate([out_grads, head_rows.T], axis=1),
        offset,
        0,
    )
    small_grad = jnp.concatenate([in_grads, placed, full_rows.T], axis=1)
    rkv_sum = scattered(jnp.concatenate(rkv_grad, axis=1))
    small_sum = scattered(
        jnp.pad(small_grad, ((0, 0), (0, packed - small_rows)))
    )
    low_shard, channel_shard = halves(small_sum, out_grads.shape[1], small_rows)
    return (
        block_output,
        input_grad,
        d_first,
        jnp.transpose(rkv_sum.reshape(-1, 3, local_width), (1, 0, 2)),
        out_shard.T,
        key_shard.T,
        value_shard.T,
        channel_shard,
        low_shard,
    )


def halves(part, ranks, used):
    total = lax.psum_scatter(part, "head", scatter_dimension=0, tiled=True).T
    low = total[: 2 * ranks]
    head_rows = total[2 * ranks : 2 * ranks + 8]
    full_rows = total[2 * ranks + 8 : used]
    return low, jnp.concatenate([full_rows, head_rows], axis=0)


def solution(mesh):
    return jax.shard_map(
        on_device,
        mesh=mesh,
        in_specs=(
            P("seq", None),
            P("seq", "head"),
            P("seq", None),
            P(),
            P(None, "seq", "head"),
            P("head", "seq"),
            P("head", "seq"),
            P("head", "seq"),
            P(None, "seq"),
            P(None, "seq"),
        ),
        out_specs=(
            P("seq", None),
            P("seq", None),
            P("seq", "head"),
            P(None, "seq", "head"),
            P("head", "seq"),
            P("head", "seq"),
            P("head", "seq"),
            P(None, ("seq", "head")),
            P(None, ("seq", "head")),
        ),
        check_vma=False,
    )
```

time: 2140 us -> 987 us (0.46)
  waiting for transfers between devices: 1300 us -> 545 us
  matrix products: 338 us -> 90.3 us
  Pallas kernels: 0 us -> 209 us
  other arithmetic: 230 us -> 39.6 us
  local copies, waits for them, and re-layouts: 189 us -> 56.9 us
  blocking collectives: 30.7 us -> 0 us
    reduce_scatter x5, waiting for transfers between devices: 721 us -> 210 us  [the longest x4 203 us: scattered(): lax.psum_scatter(full.astype(jnp.bfloat16), 'seq', scatter_dimension=0, t...]
    dot_general x139 -> x29, matrix products: 254 us -> 20.4 us  [the longest x17 10.4 us: joined(): jnp.einsum('...ij,...jk->...ik', earlier, later[..., :size, :], precision...]
    pallas_call x0 -> x4, Pallas kernels: none -> 209 us  [run(): pl.pallas_call(kernel, grid=(tokens // SPAN, width // LANES), in_specs=in...]
    all_gather x9 -> x5, waiting for transfers between devices: 389 us -> 186 us  [the longest x4 129 us: gathered(): return lax.all_gather(shard, 'seq', axis=0, tiled=True)]
    another operation x8 -> x1, other arithmetic: 166 us -> 1.09 us  [on_device(): jnp.stack([g + jnp.einsum('hij,hkj->hik', state_grad, t, precision=highes...]
    psum x3 -> x0, waiting for transfers between devices: 89.1 us -> none  [the longest x1 40.9 us: on_device(): lax.psum(dot_plain(hidden_low, value_all).astype(jnp.bfloat16), 'head')]
    ppermute x0 -> x12, waiting for transfers between devices: none -> 63.2 us  [the longest x8 59.4 us: before(): lax.ppermute(total.astype(jnp.bfloat16), 'seq', pairs).astype(jnp.float32)]
    dynamic_slice x58 -> x0, local copies, waits for them, and re-layouts: 40.7 us -> none  [the longest x20 16.8 us: one(): lax.dynamic_index_in_dim(a, source, 0, False).astype(own.dtype)]
  transfers between devices with their start and end apart: 22 -> 27, of which waited for: 20 -> 21; matrix products, arithmetic and copies ran while one was open for 12% -> 14% of each run, Pallas kernels for 0% -> 21%
where the time goes in v1:
time: 987 us; the launch traced here: 979 us
  waiting for transfers between devices  545 us (55%)
  Pallas kernels  209 us (21%)
  matrix products  90.3 us (9%)
  local copies, waits for them, and re-layouts  56.9 us (6%)
  other arithmetic  39.6 us (4%)
  starting transfers between devices  21.6 us (2%)
  between operations  16.7 us (2%)
    pallas_call x4, Pallas kernels, run(): pl.pallas_call(kernel, grid=(tokens // SPAN, width // LANES), in_specs=in...  209 us
    reduce_scatter x4, waiting for transfers between devices, scattered(): lax.psum_scatter(full.astype(jnp.bfloat16), 'seq', scatter_dimension=0, t...  203 us
    all_gather x4, waiting for transfers between devices, gathered(): return lax.all_gather(shard, 'seq', axis=0, tiled=True)  129 us
    unnamed x12, waiting for transfers between devices  79 us
    ppermute x8, waiting for transfers between devices, before(): lax.ppermute(total.astype(jnp.bfloat16), 'seq', pairs).astype(jnp.float32)  59.4 us
    all_gather x1, waiting for transfers between devices, on_device(): rkv_all = lax.all_gather(w_rkv, 'seq', axis=1, tiled=True)  56.6 us
    unnamed x355, local copies, waits for them, and re-layouts  33.3 us
    dot_general x18, matrix products, dot_tokens(): lax.dot_general(left, right, (((0,), (0,)), ((), ())), preferred_element_...  25.1 us
  transfers between devices with their start and end apart: 27, of which 21 were waited for; matrix products, arithmetic and copies ran while one was open for 14% of the time, Pallas kernels for 21%

profile of v1, /device:TPU:10, one launch (start us, length us, event | category | flops | bytes accessed | tf_op | source)
XLA Modules:
  0.0 979.1 jit_solution(15771669890552783207)
XLA Ops:
  17.2 50.9 %all-gather.6.cloned.1.call-done = bf16[1024,640]{1,0:T(8,128)(2,1)} async-done(((bf16[64,640]{1,0:T(8,128)(2,1)}), bf16[1024,640]{1,0:T(8,128)(2,1)}) %all-gather.6.cloned.1.call-update) | async-done | bytes 1310736 | tf_op jit(solution)/shard_map/all_gather | solution.py:336
  70.5 3.5 collective-permute-start
  82.6 56.6 %all-gather.8.cloned.1.call-done = bf16[3,1024,512]{2,1,0:T(8,128)(2,1)} async-done(((bf16[3,64,512]{2,1,0:T(8,128)(2,1)}), bf16[3,1024,512]{2,1,0:T(8,128)(2,1)}) %all-gather.8.cloned.1.call-update) | async-done | bytes 3145744 | tf_op jit(solution)/shard_map/all_gather | solution.py:480
  144.7 57.2 %shard_map.169 = (f32[4,8,64,64]{3,2,1,0:T(8,128)S(1)}, f32[4,8,128,64]{3,2,1,0:T(8,128)S(1)}, f32[256,512]{1,0:T(8,128)S(1)}, f32[256,512]{1,0:T(8,128)S(1)}) custom-call(f32[256,512]{1,0:T(8,128)S(1)} %fusion.36.r, f32[256,512]{1,0:T(8,128)S(1)} %fusion.38.k, f32[256,512]{1,0:T(8,128)S(1)} %fusion.40.v, bf16[256,512]{1,0:T(8,128)(2,1)S(1)} %copy-done.19, ...), custom_call_target="tpu_custom_call" | custom-call | flops 2000000000 | bytes 6848512 | tf_op jit(solution)/shard_map/pallas_call | solution.py:293
  207.8 7.3 collective-permute-done.1
  216.9 6.7 collective-permute-done.2
  225.1 13.4 %collective-permute-done.3 = bf16[8,128,64]{2,1,0:T(8,128)(2,1)S(1)} collective-permute-done((bf16[8,128,64]{2,1,0:T(8,128)(2,1)S(1)}, bf16[8,128,64]{2,1,0:T(8,128)(2,1)S(1)}, u32[]{:S(2)}, u32[]{:S(2)}) %collective-permute-start.3) | collective-permute-done | bytes 131104 | tf_op jit(solution)/shard_map/ppermute | solution.py:319
  239.2 3.1 collective-permute-start.4
  242.7 8.2 collective-permute-done.4
  252.8 11.8 %shard_map.170 = bf16[256,512]{1,0:T(8,128)(2,1)S(1)} custom-call(f32[256,512]{1,0:T(8,128)S(1)} %fusion.36.r, f32[256,512]{1,0:T(8,128)S(1)} %fusion.38.k, f32[256,512]{1,0:T(8,128)S(1)} %fusion.40.v, bf16[256,512]{1,0:T(8,128)(2,1)S(1)} %copy-done.19, f32[256,512]{1,0:T(8,128)S(1)} %convolution_add_fusion.6.a, f32[256,512]{1,0:T(8,128)S(1)} %convolution_add_fusion.5.m, ...), custom_call_target="tpu_custom_call" | custom-call | flops 100000000 | bytes 9994240 | tf_op jit(solution)/shard_map/pallas_call | solution.py:293
  271.4 3.4 collective-permute-done.6
  276.1 6.0 all-gather.12.cloned.1.call-done
  282.1 4.9 convolution_maximum_fusion
  287.0 72.5 %all-gather.14.cloned.1.call-done = bf16[1024,2048]{1,0:T(8,128)(2,1)} async-done(((bf16[64,2048]{1,0:T(8,128)(2,1)}), bf16[1024,2048]{1,0:T(8,128)(2,1)}) %all-gather.14.cloned.1.call-update) | async-done | bytes 4194320 | tf_op jit(solution)/shard_map/all_gather | solution.py:336
  359.5 4.4 fusion.1
  379.5 5.0 convert_bitcast_fusion
  384.5 6.5 copy.352
  398.0 26.8 %shard_map.171 = f32[4,8,64,64]{3,2,1,0:T(8,128)S(1)} custom-call(f32[256,512]{1,0:T(8,128)S(1)} %copy-done.10, f32[256,512]{1,0:T(8,128)S(1)} %copy-done.13, f32[256,512]{1,0:T(8,128)S(1)} %copy-done.7, bf16[256,512]{1,0:T(8,128)(2,1)S(1)} %copy-done.19, f32[256,512]{1,0:T(8,128)S(1)} %convolution_add_fusion.6.a, f32[256,512]{1,0:T(8,128)S(1)} %convolution_add_fusion.5.m, ...), custom_call_target="tpu_custom_call" | custom-call | flops 100000000 | bytes 11042816 | tf_op jit(solution)/shard_map/pallas_call | solution.py:293
  428.9 3.3 convolution_convert_fusion
  434.1 4.9 collective-permute-done.10
  443.5 5.8 collective-permute-done.11
  452.3 4.7 collective-permute-done.12
  457.7 2.9 collective-permute-start.13
  461.0 8.5 collective-permute-done.13
  475.1 76.4 %reduce-scatter.19.cloned.1.call-done = bf16[64,2048]{1,0:T(8,128)(2,1)} async-done(((bf16[1024,2048]{1,0:T(8,128)(2,1)}), bf16[64,2048]{1,0:T(8,128)(2,1)}) %reduce-scatter.19.cloned.1.call-update) | async-done | bytes 262160
  563.7 113.1 %shard_map.172 = (bf16[256,512]{1,0:T(8,128)(2,1)S(1)}, bf16[256,512]{1,0:T(8,128)(2,1)S(1)}, bf16[256,512]{1,0:T(8,128)(2,1)S(1)}, f32[256,512]{1,0:T(8,128)}, ...) custom-call(f32[256,512]{1,0:T(8,128)S(1)} %copy-done.11, ...), custom_call_target="tpu_custom_call" | custom-call | flops 4000000000 | bytes 12091392 | tf_op jit(solution)/shard_map/pallas_call | solution.py:293
  737.7 4.3 fusion.30
  742.4 2.7 concatenate.118
  746.4 68.6 %reduce-scatter.15.cloned.1.call-done = bf16[64,640]{1,0:T(8,128)(2,1)} async-done(((bf16[1024,640]{1,0:T(8,128)(2,1)}), bf16[64,640]{1,0:T(8,128)(2,1)}) %reduce-scatter.15.cloned.1.call-update) | async-done | bytes 81936 | tf_op jit(solution)/shard_map/reduce_scatter | solution.py:340
  816.7 2.8 pad_maximum_fusion
  826.9 6.3 reduce-scatter.17.cloned.1.call-done
  835.6 134.6 %reduce-scatter.13.cloned.1.call-done = bf16[64,1536]{1,0:T(8,128)(2,1)} async-done(((bf16[1024,1536]{1,0:T(8,128)(2,1)}), bf16[64,1536]{1,0:T(8,128)(2,1)}) %reduce-scatter.13.cloned.1.call-update) | async-done | bytes 196624 | tf_op jit(solution)/shard_map/reduce_scatter | solution.py:340
  (585 shorter events, 174.9 us)
Async XLA Ops:
  7.2 60.9 %all-gather.6.cloned.1.call-start = ((), (), s32[]{:S(2)}) async-start(), calls=%async_computation.6 | async-start | bytes 1392640 | tf_op jit(solution)/shard_map/all_gather | solution.py:336
  9.7 129.5 %all-gather.8.cloned.1.call-start = ((), (), s32[]{:S(2)}) async-start(), calls=%async_computation.7 | async-start | bytes 3342336 | tf_op jit(solution)/shard_map/all_gather | solution.py:480
  10.5 254.2 %all-gather.10.cloned.1.call-start = ((), (), s32[]{:S(2)}) async-start(), calls=%async_computation.8 | async-start | bytes 1114112 | tf_op jit(solution)/shard_map/all_gather | solution.py:336
  11.2 270.9 %all-gather.12.cloned.1.call-start = ((), (), s32[]{:S(2)}) async-start(), calls=%async_computation.9 | async-start | bytes 4456448 | tf_op jit(solution)/shard_map/all_gather | solution.py:336
  11.8 347.7 %all-gather.14.cloned.1.call-start = ((), (), s32[]{:S(2)}) async-start(), calls=%async_computation.10 | async-start | bytes 4456448 | tf_op jit(solution)/shard_map/all_gather | solution.py:336
  12.4 461.3 %reduce-scatter.11.cloned.1.call-start = ((), (), s32[]{:S(2)}) async-start(), calls=%async_computation.12 | async-start | bytes 1114112 | tf_op jit(solution)/shard_map/reduce_scatter | solution.py:340
  70.5 5.5 collective-permute-start
  81.0 317.0 %copy-start = (f32[256,512]{1,0:T(8,128)}, f32[256,512]{1,0:T(8,128)S(1)}, u32[]{:S(2)}) copy-start(f32[256,512]{1,0:T(8,128)S(1)} %convolution_add_fusion.5.m) | copy-start | bytes 1572868
  82.6 123.9 %copy-start.111 = (f32[256,128]{1,0:T(8,128)}, f32[256,128]{1,0:T(8,128)S(1)}, u32[]{:S(2)}) copy-start(f32[256,128]{1,0:T(8,128)S(1)} %fusion.27) | copy-start | bytes 393220
  140.9 111.8 %copy-start.6 = (f32[256,512]{1,0:T(8,128)}, f32[256,512]{1,0:T(8,128)S(1)}, u32[]{:S(2)}) copy-start(f32[256,512]{1,0:T(8,128)S(1)} %fusion.40.v) | copy-start | bytes 1572868
  142.8 109.9 %copy-start.9 = (f32[256,512]{1,0:T(8,128)}, f32[256,512]{1,0:T(8,128)S(1)}, u32[]{:S(2)}) copy-start(f32[256,512]{1,0:T(8,128)S(1)} %fusion.36.r) | copy-start | bytes 1572868
  205.9 9.3 collective-permute-start.1
  207.8 190.2 %copy-start.2 = (f32[256,512]{1,0:T(8,128)}, f32[256,512]{1,0:T(8,128)S(1)}, u32[]{:S(2)}) copy-start(f32[256,512]{1,0:T(8,128)S(1)} %fusion.110.g) | copy-start | bytes 1572868
  215.8 7.7 collective-permute-start.2
  224.3 14.1 %collective-permute-start.3 = (bf16[8,128,64]{2,1,0:T(8,128)(2,1)S(1)}, bf16[8,128,64]{2,1,0:T(8,128)(2,1)S(1)}, u32[]{:S(2)}, u32[]{:S(2)}) collective-permute-start(bf16[8,128,64]{2,1,0:T(8,128)(2,1)S(1)} %get-tuple-element.170), channel_id=1, source_target_pairs={{0,8},{2,10},{4,12},{6,14},{8,0},{10,2},{12,4},{14,6},{16,24},{18,... | collective-permute-start | bytes 393224 | tf_op jit(solution)/shard_map/ppermute | solution.py:319
  239.2 11.7 %collective-permute-start.4 = (bf16[8,128,64]{2,1,0:T(8,128)(2,1)S(1)}, bf16[8,128,64]{2,1,0:T(8,128)(2,1)S(1)}, u32[]{:S(2)}, u32[]{:S(2)}) collective-permute-start(bf16[8,128,64]{2,1,0:T(8,128)(2,1)S(1)} %fusion.11), channel_id=1, source_target_pairs={{0,16},{2,18},{4,20},{6,22},{8,24},{10,26},{12,28},{14,30},{16,0},... | collective-permute-start | bytes 393224 | tf_op jit(solution)/shard_map/ppermute | solution.py:319
  266.4 2.0 collective-permute-start.5
  269.3 5.5 collective-permute-start.6
  365.5 6.5 collective-permute-start.8
  369.6 3.0 collective-permute-start.7
  375.0 2.0 collective-permute-start.9
  379.5 172.1 %reduce-scatter.19.cloned.1.call-start = ((), (), s32[]{:S(2)}) async-start(), calls=%async_computation.16 | async-start | bytes 4456448
  391.1 315.3 %reduce-scatter.9.cloned.1.call-start = ((), (), s32[]{:S(2)}) async-start(), calls=%async_computation.11 | async-start | bytes 4456448 | tf_op jit(solution)/shard_map/reduce_scatter | solution.py:340
  428.6 10.4 %collective-permute-start.10 = (bf16[8,128,64]{2,1,0:T(8,128)(2,1)}, bf16[8,128,64]{2,1,0:T(8,128)(2,1)}, u32[]{:S(2)}, u32[]{:S(2)}) collective-permute-start(bf16[8,128,64]{2,1,0:T(8,128)(2,1)} %fusion.49), channel_id=1, source_target_pairs={{0,2},{2,0},{4,6},{6,4},{8,10},{10,8},{12,14},{14,12},{16,18},{18,... | collective-permute-start | bytes 393224 | tf_op jit(solution)/shard_map/ppermute | solution.py:319
  432.9 382.2 %reduce-scatter.15.cloned.1.call-start = ((), (), s32[]{:S(2)}) async-start(), calls=%async_computation.14 | async-start | bytes 1392640 | tf_op jit(solution)/shard_map/reduce_scatter | solution.py:340
  441.6 7.7 collective-permute-start.11
  450.1 6.8 collective-permute-start.12
  457.7 11.8 %collective-permute-start.13 = (bf16[8,128,64]{2,1,0:T(8,128)(2,1)S(1)}, bf16[8,128,64]{2,1,0:T(8,128)(2,1)S(1)}, u32[]{:S(2)}, u32[]{:S(2)}) collective-permute-start(bf16[8,128,64]{2,1,0:T(8,128)(2,1)S(1)} %fusion.12), channel_id=1, source_target_pairs={{0,16},{2,18},{4,20},{6,22},{8,24},{10,26},{12,28},{14,30},{16,0},... | collective-permute-start | bytes 393224 | tf_op jit(solution)/shard_map/ppermute | solution.py:319
  714.8 22.8 %collective-permute-start.14 = (f32[1,1024]{1,0:T(1,128)}, f32[1,1024]{1,0:T(1,128)}, u32[]{:S(2)}, u32[]{:S(2)}) collective-permute-start(f32[1,1024]{1,0:T(1,128)} %slice.502), channel_id=1, source_target_pairs={{2,0},{4,2},{6,4},{8,6},{10,8},{12,10},{14,12},{16,14},{18,16},{20... | collective-permute-start | bytes 12296 | tf_op jit(solution)/shard_map/ppermute | solution.py:27
  746.4 86.9 %reduce-scatter.17.cloned.1.call-start = ((), (), s32[]{:S(2)}) async-start(), calls=%async_computation.15 | async-start | bytes 245760 | tf_op jit(solution)/shard_map/reduce_scatter | solution.py:651
  816.6 153.6 %reduce-scatter.13.cloned.1.call-start = ((), (), s32[]{:S(2)}) async-start(), calls=%async_computation.13 | async-start | bytes 3342336 | tf_op jit(solution)/shard_map/reduce_scatter | solution.py:340
  822.2 2.3 collective-permute-start.15
  (169 other events, 1792.5 us)
Sparse Core Ops, SparseCore 0:
  11.3 56.7 all-gather.5
  70.9 68.3 all-gather.7
  142.0 53.0 all-gather.9
  197.7 84.3 all-gather.11
  284.7 74.7 all-gather.13
  379.6 68.1 reduce-scatter.10
  450.2 101.3 reduce-scatter.18
  554.0 94.2 reduce-scatter.8
  746.5 68.5 reduce-scatter.14
  818.4 14.8 reduce-scatter.16
  839.0 131.1 reduce-scatter.12
